TPU v7x, 256 devices: a whole 4x4x8 slice. The times are simulated.
256 devices in a mesh: tile: 8 (over y, core), acq: 32 (over x, z).
Axes of the slice: x: 4, y: 4, z: 8, core: 2. Of those that a mesh axis runs over, the one named last changes fastest.
Arguments:
- complex_stack: float32 [128, 2, 1024, 512], P('acq', None, 'tile'), may hold values from -3 to 3, as said below
- pair_list: int32 [256, 2], P('acq'), may hold values from -1 to 127, as said below
- stack_order: int32 [128], replicated, may hold values from 0 to 127, as said below
- references: int32 [4], replicated, may hold values from 0 to 127, as said below
Outputs:
- series: float32 [131072, 128], P(('tile', 'acq'))
- coherence: float32 [256, 256, 512], P('acq', 'tile')
Inputs may be any that keep to these rules, and one draw needn't show every extreme that they name: `complex_stack`: real and imaginary parts of complex values whose magnitude lies in 0.3 to 3 and whose phase lies in -pi/6 to pi/6. `pair_list`: rows p * 8 to p * 8 + 7 belong to index p of acq; each live row names a secondary stored on that index and a reference number; the live rows of a block come first and no (reference number, secondary) occurs twice; empty rows hold -1 in both columns; every block has one live row or more and some block is all live. `stack_order`: A permutation of the acquisition numbers. `references`: distinct acquisition numbers; acquisitions 0 and 127 are among them.
All inputs are finite; a program needn't handle non-finite values.
Results may differ from a plain program's by a relative error of at most 0.0003.
Values sent between devices are 32-bit elements; how exact they have to be, the bound alone decides.
A program may use at most 64 MiB of HBM per device.

v0:
```python
import jax
import jax.numpy as jnp
from jax import lax
from jax.sharding import PartitionSpec as P

NREF = 4
LOOKS = 4


def broadcast(value, axis, source):
    kept = jnp.where(lax.axis_index(axis) == source, value, 0).astype(value.dtype)
    return lax.psum(kept, axis)


def with_halo(block, sides, width):
    for axis, dim in sides:
        count = lax.axis_size(axis)
        forward = [(i, i + 1) for i in range(count - 1)]
        backward = [(target, source) for source, target in forward]
        low = lax.ppermute(
            lax.slice_in_dim(block, block.shape[dim] - width, None, axis=dim), axis, forward
        )
        high = lax.ppermute(lax.slice_in_dim(block, 0, width, axis=dim), axis, backward)
        block = jnp.concatenate([low, block, high], axis=dim)
    return block


def window_sum(padded):
    inner_rows = padded.shape[-2] - 2
    row_total = (
        padded[..., 0:inner_rows, :]
        + padded[..., 1 : inner_rows + 1, :]
        + padded[..., 2 : inner_rows + 2, :]
    )
    columns = row_total.shape[-1]
    spread = jnp.pad(row_total, [(0, 0)] * (row_total.ndim - 1) + [(2, 2)])
    return (
        spread[..., 0:columns]
        + spread[..., 1 : columns + 1]
        + spread[..., 2 : columns + 2]
        + spread[..., 3 : columns + 3]
        + spread[..., 4 : columns + 4]
    )


def slot_lookup(wanted, stack_order):
    numbers = jnp.arange(stack_order.shape[0], dtype=jnp.int32)
    found = jnp.where(stack_order[None, :] == wanted[:, None], numbers[None, :], 0)
    return jnp.sum(found, axis=1)


def local(complex_stack, pair_list, stack_order, references):
    per_device = complex_stack.shape[0]
    height = complex_stack.shape[2]
    columns = complex_stack.shape[3]
    slot_count = pair_list.shape[0]
    my_index = lax.axis_index("acq")
    ref_slot = slot_lookup(references, stack_order)
    ref_owner = ref_slot // per_device
    ref_local = ref_slot % per_device
    tiles = []
    for which in range(NREF):
        own_tile = lax.dynamic_index_in_dim(complex_stack, ref_local[which], 0, keepdims=False)
        tiles.append(broadcast(own_tile, "acq", ref_owner[which]))
    ref_stack = jnp.stack(tiles)
    kinds = pair_list[:, 0]
    living = kinds >= 0
    sec_slot = slot_lookup(pair_list[:, 1], stack_order)
    sec_local = jnp.where(living, sec_slot - my_index * per_device, 0)
    primary = jnp.take(ref_stack, jnp.maximum(kinds, 0), axis=0)
    second = jnp.take(complex_stack, sec_local, axis=0)
    looked = height // LOOKS

    def multilook(values):
        return values.reshape(slot_count, looked, LOOKS, columns).sum(axis=2)

    first_real, first_imag = (primary[:, 0], primary[:, 1])
    second_real, second_imag = (second[:, 0], second[:, 1])
    look_real = multilook(first_real * second_real + first_imag * second_imag)
    look_imag = multilook(first_imag * second_real - first_real * second_imag)
    power_first = multilook(first_real * first_real + first_imag * first_imag)
    power_second = multilook(second_real * second_real + second_imag * second_imag)
    stacked = jnp.stack([look_real, look_imag, power_first, power_second], axis=1)
    padded = with_halo(stacked, (("tile", 2),), 1)
    boxed = window_sum(padded)
    coherence = jnp.sqrt(boxed[:, 0] ** 2 + boxed[:, 1] ** 2) / jnp.sqrt(boxed[:, 2] * boxed[:, 3])
    coherence = jnp.where(living[:, None, None], coherence, 0.0)
    phase = jnp.where(living[:, None, None], jnp.arctan2(look_imag, look_real), 0.0)
    all_pairs = lax.all_gather(pair_list, "acq", axis=0, tiled=True)
    all_kinds = all_pairs[:, 0]
    all_living = all_kinds >= 0
    ref_acq = references[jnp.maximum(all_kinds, 0)]
    sec_acq = jnp.maximum(all_pairs[:, 1], 0)
    numbers = jnp.arange(stack_order.shape[0], dtype=jnp.int32)
    design = (numbers[None, :] == ref_acq[:, None]).astype(jnp.float32) - (
        numbers[None, :] == sec_acq[:, None]
    ).astype(jnp.float32)
    design = jnp.where(all_living[:, None], design, 0.0)
    normal = jnp.dot(design.T, design, precision=lax.Precision.HIGHEST) + jnp.eye(
        stack_order.shape[0], dtype=jnp.float32
    )
    factor = jnp.linalg.cholesky(normal)
    solver = jax.scipy.linalg.cho_solve((factor, True), design.T)
    series = lax.dot_general(
        lax.all_to_all(phase, "acq", split_axis=1, concat_axis=0, tiled=True)[:, 0, :],
        solver,
        (((0,), (1,)), ((), ())),
        precision=lax.Precision.HIGHEST,
    )
    return (series, coherence)


def solution(mesh):
    return jax.shard_map(
        local,
        mesh=mesh,
        in_specs=(P("acq", None, "tile", None), P("acq", None), P(), P()),
        out_specs=(P(("tile", "acq"), None), P("acq", "tile", None)),
        check_vma=False,
    )
```

profile of v0, /device:TPU:1, one launch (start us, length us, event | category | flops | bytes accessed | tf_op | source)
XLA Modules:
  0.0 264.8 jit_solution(18212465917055404741)
XLA Ops:
  7.2 0.9 select_reduce_fusion.2
  18.8 3.0 %dynamic-slice_select_fusion.3 = (f32[1,2,128,512]{3,2,1,0:T(8,128)}, f32[1,2,128,512]{3,2,1,0:T(8,128)}, f32[1,2,128,512]{3,2,1,0:T(8,128)}, f32[1,2,128,512]{3,2,1,0:T(8,128)}) fusion(f32[4,2,128,512]{3,2,1,0:T(8,128)} %param.6, s32[]{:T(128)S(6)} %select_n.102, pred[]{:T(512)S(6)} %eq.77, s32[]{:T(128)S(6)} %select_n.110, pred[]{:T(512)S(6)} %eq.79, ...), kind=kLoop, calls=%fused_computation.43 | loop fusion | flops 524288 | bytes 4194324 | tf_op jit(solution)/shard_map/jit(_where)/select_n | solution.py:11
  22.6 0.7 copy-done
  23.4 2.7 %gather_fusion.1 = f32[8,2,128,512]{3,2,1,0:T(8,128)} fusion(f32[4,2,128,512]{3,2,1,0:T(8,128)S(1)} %copy-done, s32[1024]{0:T(1024)S(1)} %pad_clamp_fusion), kind=kCustom, calls=%fused_computation.1.clone | custom fusion | bytes 8388640 | tf_op jit(solution)/shard_map/jit(_take)/gather | solution.py:71
  26.1 39.6 %all-gather = s32[32,8,2]{1,2,0:T(2,128)S(1)} all-gather(s32[1,8,2]{1,2,0:T(2,128)S(1)} %bitcast.73), channel_id=1, replica_groups=mesh['tile'=8,'acq'=32] {'acq'}, dimensions={0}, use_global_device_ids=true | all-gather | bytes 2112 | tf_op jit(solution)/shard_map/all_gather | solution.py:89
  66.4 2.5 compare_select_fusion
  69.5 4.9 %broadcast_select_fusion = f32[8,2,128,512]{3,2,1,0:T(8,128)} fusion(f32[8,2,128,512]{3,2,1,0:T(8,128)} %gather_fusion.1, pred[8]{0:T(512)(128)(4,1)S(1)} %get-tuple-element.25), kind=kLoop, calls=%fused_computation.22 | loop fusion | flops 1048576 | bytes 8388616 | tf_op jit(solution)/shard_map/jit(_take)/select_n | solution.py:71
  74.4 101.7 %all-reduce.4.cloned.1.call-done = (f32[1,2,128,512]{3,2,1,0:T(8,128)}, f32[1,2,128,512]{3,2,1,0:T(8,128)}, f32[1,2,128,512]{3,2,1,0:T(8,128)}, f32[1,2,128,512]{3,2,1,0:T(8,128)}) async-done(((f32[1,2,128,512]{3,2,1,0:T(8,128)}, f32[1,2,128,512]{3,2,1,0:T(8,128)}, f32[1,2,128,512]{3,2,1,0:T(8,128)}, f32[1,2,128,512]{3,2,1,0:T(8,128)}), (f32[1,2,128,512]{3,2,1,0:T(8,128)}, f32[1,2,128,512]{3,2,1,0:T(8,128)}, ...) | async-done | bytes 2097168 | tf_op jit(solution)/shard_map/psum | solution.py:12
  176.0 1.8 pad_maximum_fusion.8
  177.8 2.8 %gather_fusion = f32[8,2,128,512]{3,2,1,0:T(8,128)} fusion(f32[4,2,128,512]{3,2,1,0:T(8,128)S(1)} %pad_maximum_fusion.8, s32[1024]{0:T(1024)S(1)} %pad_clamp_fusion.1), kind=kCustom, calls=%fused_computation.clone | custom fusion | bytes 8388640 | tf_op jit(solution)/shard_map/jit(_take)/gather | solution.py:70
  180.6 2.9 %broadcast_select_fusion.1 = f32[8,2,128,512]{3,2,1,0:T(8,128)S(1)} fusion(f32[8,2,128,512]{3,2,1,0:T(8,128)} %gather_fusion, pred[8]{0:T(512)(128)(4,1)S(1)} %get-tuple-element.9), kind=kLoop, calls=%fused_computation.23 | loop fusion | flops 1048576 | bytes 8388616 | tf_op jit(solution)/shard_map/jit(_take)/select_n | solution.py:70
  184.1 4.8 %multiply_add_fusion.2 = (f32[8,1,128,512]{3,2,1,0:T(8,128)}, f32[8,1,128,512]{3,2,1,0:T(8,128)}, f32[8,1,128,512]{3,2,1,0:T(8,128)}, f32[8,1,128,512]{3,2,1,0:T(8,128)}) fusion(f32[8,2,128,512]{3,2,1,0:T(8,128)S(1)} %copy-done.1, f32[8,2,128,512]{3,2,1,0:T(8,128)S(1)} %broadcast_select_fusion.1), kind=kLoop, calls=%fused_computation.26 | loop fusion | flops 6291456 | bytes 16777216 | tf_op jit(solution)/shard_map/add | solution.py:79
  188.9 1.9 add.117
  190.7 2.9 %sub.28 = f32[8,32,4,512]{3,2,1,0:T(4,128)} reshape(f32[8,1,128,512]{3,2,1,0:T(8,128)} %get-tuple-element.14) | data formatting | bytes 4194304 | tf_op jit(solution)/shard_map/sub | solution.py:80
  193.6 1.3 reduce_sum.57
  194.9 2.9 %reduce_sum.56 = f32[8,32,512]{2,1,0:T(8,128)S(1)} reduce(f32[8,32,4,512]{3,2,1,0:T(4,128)} %sub.28, f32[]{:T(128)} %constant.104.clone.1), dimensions={2}, to_apply=%region_6.8 | reduce | flops 393216 | bytes 2621444 | tf_op jit(solution)/shard_map/reduce_sum | solution.py:75
  197.8 1.9 add.122
  199.7 2.2 reduce_sum.58
  201.8 1.9 add.124
  203.7 2.2 reduce_sum.59
  205.8 1.5 pad_maximum_fusion.9
  207.5 7.6 %collective-permute-start = (f32[8,4,1,512]{3,2,0,1:T(1,128)S(1)}, f32[8,4,1,512]{3,2,0,1:T(1,128)S(1)}, u32[]{:S(2)}, u32[]{:S(2)}) collective-permute-start(f32[8,4,1,512]{3,2,0,1:T(1,128)S(1)} %get-tuple-element.17), channel_id=1, source_target_pairs={{0,32},{32,64},{64,96},{96,128},{128,160},{160,192},{192,224},{1,3... | collective-permute-start | bytes 196616 | tf_op jit(solution)/shard_map/ppermute | solution.py:20
  215.1 2.1 collective-permute-start.1
  217.3 3.4 %collective-permute-done.1 = f32[8,4,1,512]{3,2,0,1:T(1,128)S(1)} collective-permute-done((f32[8,4,1,512]{3,2,0,1:T(1,128)S(1)}, f32[8,4,1,512]{3,2,0,1:T(1,128)S(1)}, u32[]{:S(2)}, u32[]{:S(2)}) %collective-permute-start.1) | collective-permute-done | bytes 65568 | tf_op jit(solution)/shard_map/ppermute | solution.py:23
  220.6 0.9 fusion.4
  221.5 2.2 fusion.3
  223.8 1.8 fusion.9
  225.6 1.1 copy.16
  226.7 6.0 %all-to-all-start = ((f32[8,32,512]{2,0,1:T(8,128)}), f32[8,32,512]{2,0,1:T(8,128)S(1)}, u32[]{:S(2)}, u32[]{:S(2)}) async-start(f32[8,32,512]{2,0,1:T(8,128)} %copy.16), calls=%async_computation | async-start | bytes 1048576 | tf_op jit(solution)/shard_map/all_to_all | solution.py:105
  232.7 11.7 %cholesky.17 = f32[128,128]{1,0:T(8,128)S(1)} custom-call(f32[128,128]{1,0:T(8,128)S(1)} %fusion.21), custom_call_target="Cholesky" | custom-call | tf_op jit(solution)/shard_map/jit(cholesky)/cholesky | solution.py:102
  245.7 9.8 %custom-call.10 = f32[1,128,128]{1,2,0:T(8,128)S(1)} custom-call(f32[1,128,128]{2,1,0:T(8,128)S(1)} %fusion.16), custom_call_target="InvertDiagBlocksLowerTriangular" | custom-call | tf_op jit(solution)/shard_map/jit(_cho_solve)/triangular_solve | solution.py:103
  256.2 1.7 fusion.12
  (38 shorter events, 5.7 us)
Async XLA Ops:
  7.2 168.9 %all-reduce.4.cloned.1.call-start = ((), (), s32[]{:S(2)}) async-start(), calls=%async_computation.1 | async-start | bytes 4194304 | tf_op jit(solution)/shard_map/psum | solution.py:12
  21.8 0.7 copy-start.5
  21.8 0.7 copy-start.6
  21.8 1.6 copy-start
  23.4 42.5 %copy-start.4 = (s32[4]{0:T(128)S(1)}, s32[4]{0:T(128)}, u32[]{:S(2)}) copy-start(s32[4]{0:T(128)} %param.9) | copy-start | bytes 52
  180.6 3.4 %copy-start.1 = (f32[8,2,128,512]{3,2,1,0:T(8,128)S(1)}, f32[8,2,128,512]{3,2,1,0:T(8,128)}, u32[]{:S(2)}) copy-start(f32[8,2,128,512]{3,2,1,0:T(8,128)} %broadcast_select_fusion) | copy-start | bytes 12582916
  205.8 14.8 %copy-start.2 = (f32[8,32,512]{2,1,0:T(8,128)S(1)}, f32[8,32,512]{2,1,0:T(8,128)}, u32[]{:S(2)}) copy-start(f32[8,32,512]{2,1,0:T(8,128)} %reduce_sum.58) | copy-start | bytes 1572868
  205.8 14.8 %copy-start.3 = (f32[8,32,512]{2,1,0:T(8,128)S(1)}, f32[8,32,512]{2,1,0:T(8,128)}, u32[]{:S(2)}) copy-start(f32[8,32,512]{2,1,0:T(8,128)} %reduce_sum.59) | copy-start | bytes 1572868
  207.5 9.8 %collective-permute-start = (f32[8,4,1,512]{3,2,0,1:T(1,128)S(1)}, f32[8,4,1,512]{3,2,0,1:T(1,128)S(1)}, u32[]{:S(2)}, u32[]{:S(2)}) collective-permute-start(f32[8,4,1,512]{3,2,0,1:T(1,128)S(1)} %get-tuple-element.17), channel_id=1, source_target_pairs={{0,32},{32,64},{64,96},{96,128},{128,160},{160,192},{192,224},{1,3... | collective-permute-start | bytes 196616 | tf_op jit(solution)/shard_map/ppermute | solution.py:20
  215.1 5.6 %collective-permute-start.1 = (f32[8,4,1,512]{3,2,0,1:T(1,128)S(1)}, f32[8,4,1,512]{3,2,0,1:T(1,128)S(1)}, u32[]{:S(2)}, u32[]{:S(2)}) collective-permute-start(f32[8,4,1,512]{3,2,0,1:T(1,128)S(1)} %get-tuple-element.18), channel_id=1, source_target_pairs={{32,0},{64,32},{96,64},{128,96},{160,128},{192,160},{224,192},{33,... | collective-permute-start | bytes 196616 | tf_op jit(solution)/shard_map/ppermute | solution.py:23
  226.7 29.6 %all-to-all-start = ((f32[8,32,512]{2,0,1:T(8,128)}), f32[8,32,512]{2,0,1:T(8,128)S(1)}, u32[]{:S(2)}, u32[]{:S(2)}) async-start(f32[8,32,512]{2,0,1:T(8,128)} %copy.16), calls=%async_computation | async-start | bytes 1048576 | tf_op jit(solution)/shard_map/all_to_all | solution.py:105
Sparse Core Ops, SparseCore 0:
  21.9 154.0 all-reduce.3
where the time goes:
time: 266 us; the launch traced here: 265 us
  waiting for transfers between devices  105 us (39%)
  other arithmetic  58.6 us (22%)
  blocking collectives  39.6 us (15%)
  between operations  24.3 us (9%)
  local copies, waits for them, and re-layouts  18.6 us (7%)
  starting transfers between devices  15.7 us (6%)
  matrix products  3 us (1%)
    psum x1, waiting for transfers between devices, broadcast(): return lax.psum(kept, axis)  102 us
    all_gather x1, blocking collectives, local(): all_pairs = lax.all_gather(pair_list, 'acq', axis=0, tiled=True)  39.6 us
    another operation x3, other arithmetic, local(): factor = jnp.linalg.cholesky(normal)  12.4 us
    another operation x2, other arithmetic, local(): solver = jax.scipy.linalg.cho_solve((factor, True), design.T)  10.5 us
    reduce_sum x4, other arithmetic, multilook(): return values.reshape(slot_count, looked, LOOKS, columns).sum(axis=2)  8.47 us
    ppermute x1, starting transfers between devices, with_halo(): lax.ppermute(lax.slice_in_dim(block, block.shape[dim] - width, None, axis...  7.58 us
    all_to_all x1, starting transfers between devices, local(): lax.all_to_all(phase, 'acq', split_axis=1, concat_axis=0, tiled=True)  5.96 us
  transfers between devices with their start and end apart: 4, of which 2 were waited for; matrix products, arithmetic and copies ran while one was open for 13% of the time, Pallas kernels for 0%

commit v1 on v0

v1 whole, which is shorter than its diff:
```python
import functools

import jax
import jax.numpy as jnp
from jax import lax
from jax.experimental import pallas as pl
from jax.experimental.pallas import tpu as pltpu
from jax.sharding import PartitionSpec as P

MESH = pl.DeviceIdType.MESH
HIGHEST = lax.Precision.HIGHEST
NREF = 4
LOOKS = 4
NX = 4
NZ = 8
A_DEV = 4
CAP = 8
COLS = 512
BLOCKS = 4
ROWS = 8
NACQ = 128
SLOTS = NX * CAP
ACQS = NX * A_DEV
QUANT = 2 * SLOTS + NREF + ACQS
QPAD = 88

ATAN = (
    1.0, -0.33333277702331543, 0.1999807506799698, -0.1426001638174057, 0.1093234121799469,
    -0.08349724858999252, 0.05708955600857735, -0.03035186603665352, 0.010487649589776993,
    -0.0017011701129376888,
)


def atan2(y, x):
    ax, ay = jnp.abs(x), jnp.abs(y)
    t = jnp.minimum(ax, ay) / jnp.maximum(ax, ay)
    u = t * t
    acc = jnp.full_like(u, ATAN[-1])
    for coefficient in ATAN[-2::-1]:
        acc = acc * u + coefficient
    r = acc * t
    r = jnp.where(ay > ax, jnp.pi / 2 - r, r)
    r = jnp.where(x < 0, jnp.pi - r, r)
    return jnp.where(y < 0, -r, r)


def dot(a, b, dims):
    return lax.dot_general(a, b, (dims, ((), ())), precision=HIGHEST, preferred_element_type=jnp.float32)


def make_solver(design, refs):
    lane = lax.broadcasted_iota(jnp.int32, (8, NACQ), 1)
    sub = lax.broadcasted_iota(jnp.int32, (8, NACQ), 0)
    pick = jnp.zeros((8, NACQ), jnp.float32)
    for k in range(NREF):
        pick = jnp.where((sub == k) & (lane == refs[k]), 1.0, pick)
    is_ref = jnp.sum(pick, axis=0, keepdims=True)
    other = 1.0 - is_ref
    degree = jnp.sum(design * design, axis=0, keepdims=True)
    inverse = other / (1.0 + degree)
    on_ref = dot(design, pick, ((1,), (1,)))
    normal_ref = dot(on_ref, design, ((0,), (0,))) + pick
    right = on_ref - dot(design * inverse, normal_ref, ((1,), (1,)))
    schur = dot(normal_ref, pick, ((1,), (1,))) - dot(normal_ref * inverse, normal_ref, ((1,), (1,)))
    row8 = lax.broadcasted_iota(jnp.int32, (8, 8), 0)
    col8 = lax.broadcasted_iota(jnp.int32, (8, 8), 1)
    eye8 = jnp.where(row8 == col8, 1.0, 0.0)
    left = schur + jnp.where(row8 >= NREF, eye8, 0.0)
    inv = eye8
    for k in range(NREF):
        pivot = 1.0 / left[k : k + 1, k : k + 1]
        lrow, irow = left[k : k + 1, :] * pivot, inv[k : k + 1, :] * pivot
        column = jnp.where(row8[:, 0:1] == k, 0.0, left[:, k : k + 1])
        left = jnp.where(row8 == k, lrow, left - column * lrow)
        inv = jnp.where(row8 == k, irow, inv - column * irow)
    at_ref = dot(right, inv, ((1,), (0,)))
    rest = (design - dot(at_ref, normal_ref, ((1,), (0,)))) * inverse
    return rest + dot(at_ref, pick, ((1,), (0,)))


def kernel(
    chunks, nc,
    stack_hbm, pairs, order, refs, owners, series, coherence,
    stack, ps, xa, xg, zs, zr, rf, ph, pa, info, info_s, da, xt, quant, hlo, hhi, rlo, rhi, coh,
    load_sem, s1s, s1r, i_sem, is_, ir, d2s, d2r, rs_s, rs_r, ag_s, ag_r, pa_s, pa_r, h_s, h_r, co_s, co_r, own_sem,
):
    width = COLS // nc
    tile, acq = lax.axis_index("tile"), lax.axis_index("acq")
    x, z = acq // NZ, lax.rem(acq, NZ)

    def at_x(d):
        return lax.rem(x + d, NX)

    def at_z(d):
        return lax.rem(z + d, NZ)

    def dev_x(d):
        return (tile, at_x(d) * NZ + z)

    def dev_z(d):
        return (tile, x * NZ + at_z(d))

    place = tile * NX + x

    def dev_q(d):
        q = lax.rem(place + d + 32, 32)
        return (q // NX, lax.rem(q, NX) * NZ + z)

    loads = []
    for a in range(A_DEV):
        for b in range(BLOCKS):
            copy = pltpu.make_async_copy(
                stack_hbm.at[a, :, :, pl.ds(b * 128, 128)], stack.at[a, b], load_sem.at[a, b]
            )
            copy.start()
            loads.append(copy)

    barrier = pltpu.get_barrier_semaphore()
    partners = [dev_x(d) for d in range(1, NX)] + [dev_z(d) for d in range(1, NZ)] + [dev_q(1), dev_q(-1)]
    for partner in partners:
        pl.semaphore_signal(barrier, inc=1, device_id=partner, device_id_type=MESH)

    def send(src, dst, ssem, rsem, device):
        copy = pltpu.make_async_remote_copy(
            src_ref=src, dst_ref=dst, send_sem=ssem, recv_sem=rsem, device_id=device, device_id_type=MESH
        )
        copy.start()

    def wait(ref, sem):
        pltpu.make_async_copy(ref, ref, sem).wait()

    mine = [order[acq * A_DEV + a] for a in range(A_DEV)]
    ref_no = [refs[k] for k in range(NREF)]
    is_ref = []
    for a in range(A_DEV):
        hit = jnp.int32(0)
        for k in range(NREF):
            hit = hit + jnp.where(mine[a] == ref_no[k], 1, 0)
        is_ref.append(jnp.minimum(hit, 1))
    n_ref = is_ref[0] + is_ref[1] + is_ref[2] + is_ref[3]
    position, refs_before, others_before = [], jnp.int32(0), jnp.int32(0)
    for a in range(A_DEV):
        position.append(jnp.where(is_ref[a] > 0, refs_before, n_ref + others_before))
        refs_before = refs_before + is_ref[a]
        others_before = others_before + 1 - is_ref[a]
    local = []
    for c in range(A_DEV):
        where = jnp.int32(0)
        for a in range(A_DEV):
            where = where + jnp.where(position[a] == c, a, 0)
        local.append(jnp.minimum(where, A_DEV - 1))

    lane = lax.broadcasted_iota(jnp.int32, (CAP, 128), 1)
    sub = lax.broadcasted_iota(jnp.int32, (CAP, 128), 0)
    rows = jnp.zeros((CAP, 128), jnp.float32)
    facts = jnp.zeros((CAP, 128), jnp.int32)
    for s in range(CAP):
        kind, second = pairs[s, 0], pairs[s, 1]
        live = jnp.where(kind >= 0, 1, 0)
        kind = jnp.maximum(kind, 0)
        first = refs[kind]
        spot = jnp.int32(0)
        for a in range(A_DEV):
            spot = spot + jnp.where(mine[a] == second, position[a], 0)
        spot = jnp.minimum(spot, A_DEV - 1)
        row = jnp.where(lane == first, 1.0, 0.0) - jnp.where(lane == second, 1.0, 0.0)
        row = jnp.where(live > 0, row, 0.0)
        rows = jnp.where(sub == s, row, rows)
        fact = jnp.where(lane == 0, kind, jnp.where(lane == 1, spot, jnp.where(lane == 2, live, 0)))
        facts = jnp.where(sub == s, fact, facts)
    info[x] = facts
    da[z, x] = rows

    for copy in loads:
        copy.wait()

    def arrange(c):
        a = local[c]

        def body(t, carry):
            q, part = t // 2, lax.rem(t, 2)
            for j in range(LOOKS):
                for b in range(BLOCKS):
                    h, inner = divmod(b, BLOCKS // nc)
                    ps[c, q, h, part, j, :, pl.ds(inner * 128, 128)] = stack[
                        a, b, part, pl.ds(q * (ROWS * LOOKS) + j, ROWS, stride=LOOKS), :
                    ]
            return carry

        lax.fori_loop(0, NX * 2, body, 0)

    own = []

    def landing(c):
        return xa.at[c] if c < chunks else xg.at[c]

    def send_chunk(c):
        for d in (1, 3, 2):
            send(ps.at[c, at_x(d)], landing(c).at[x], s1s.at[c], s1r.at[c], dev_x(d))
        copy = pltpu.make_async_copy(ps.at[c, x], landing(c).at[x], own_sem.at[c])
        copy.start()
        own.append(copy)

    arrange(0)
    pl.semaphore_wait(barrier, len(partners))
    for d in range(1, NX):
        send(info.at[x], info.at[x], is_, ir, dev_x(d))
        send(da.at[z, x], da.at[z, x], d2s.at[0], d2r.at[0], dev_x(d))
    send_chunk(0)
    for c in range(1, A_DEV):
        arrange(c)
        send_chunk(c)

    three = pl.ds(0, NX - 1)
    wait(info.at[three], ir)
    to_smem = pltpu.make_async_copy(info, info_s, i_sem)
    to_smem.start()
    wait(da.at[0, three], d2r.at[0])
    for d in range(1, NZ):
        send(da.at[z], da.at[z], d2s.at[1], d2r.at[1], dev_z(d))

    def arrived(c):
        wait(landing(c).at[three], s1r.at[c])
        own[c].wait()

    for c in range(chunks):
        arrived(c)

    where_ref = [(owners[k], owners[NREF + k], owners[2 * NREF + k]) for k in range(NREF)]
    seven = pl.ds(0, NZ - 1)
    for h in range(nc):
        for k in range(NREF):
            rx, _, rc = where_ref[k]
            for part in range(2):
                for j in range(LOOKS):
                    zs[h, part * LOOKS + j, k] = xa[rc, rx, h, part, j]
        for d in range(1, NZ):
            send(zs.at[h, at_z(d)], zr.at[h, z], rs_s.at[h], rs_r.at[h], dev_z(d))
        zr[h, z] = zs[h, z]

    half = NREF // 2
    low, high = pl.ds(0, half), pl.ds(half, half)
    for h in range(nc):
        wait(zr.at[h, seven], rs_r.at[h])
        for k in range(NREF):
            _, rz, _ = where_ref[k]
            rf[h, z, k] = zr[h, rz, k]
        send(rf.at[h, z], rf.at[h, z], ag_s.at[h, 0, 0], ag_r.at[h, 0, 0], dev_z(1))
        send(rf.at[h, z], rf.at[h, z], ag_s.at[h, 1, 0], ag_r.at[h, 1, 0], dev_z(7))

    def take(t, carry):
        for c in range(chunks):
            for part in range(2):
                for j in range(LOOKS):
                    xg[c, t // nc, lax.rem(t, nc), part, j] = xa[c, t // nc, lax.rem(t, nc), part, j]
        return carry

    lax.fori_loop(0, NX * nc, take, 0)
    for c in range(chunks, A_DEV):
        arrived(c)
    to_smem.wait()
    wait(da.at[seven], d2r.at[1])
    xt[...] = make_solver(da[...].reshape(NZ * NX * CAP, NACQ), ref_no)

    for step in range(1, 4):
        for h in range(nc):
            left, right = at_z(NZ - step), at_z(step)
            wait(rf.at[h, left], ag_r.at[h, 0, step - 1])
            wait(rf.at[h, right], ag_r.at[h, 1, step - 1])
            if step < 3:
                send(rf.at[h, left], rf.at[h, left], ag_s.at[h, 0, step], ag_r.at[h, 0, step], dev_z(1))
                send(rf.at[h, right], rf.at[h, right], ag_s.at[h, 1, step], ag_r.at[h, 1, step], dev_z(7))
            else:
                send(rf.at[h, left, low], rf.at[h, left, low], ag_s.at[h, 0, 3], ag_r.at[h, 0, 3], dev_z(1))
                send(rf.at[h, right, high], rf.at[h, right, high], ag_s.at[h, 1, 3], ag_r.at[h, 1, 3], dev_z(7))

    for h in range(nc):
        far = at_z(4)
        wait(rf.at[h, far, low], ag_r.at[h, 0, 3])
        wait(rf.at[h, far, high], ag_r.at[h, 1, 3])
        columns = pl.ds(h * width, width)

        def slot_body(s, carry, h=h, columns=columns):
            group, index = s // CAP, lax.rem(s, CAP)
            kind, spot, live = info_s[group, index, 0], info_s[group, index, 1], info_s[group, index, 2]
            real = imag = None
            for j in range(LOOKS):
                a, b = rf[h, j, kind], rf[h, LOOKS + j, kind]
                c, d = xg[spot, group, h, 0, j], xg[spot, group, h, 1, j]
                re, im = a * c + b * d, b * c - a * d
                real, imag = (re, im) if j == 0 else (real + re, imag + im)
            quant[s, :, columns] = real
            quant[SLOTS + s, :, columns] = imag
            phase = jnp.where(live > 0, atan2(imag, real), 0.0)
            for b in range(BLOCKS // nc):
                ph[h, b, pl.ds(s, ROWS, stride=SLOTS), :] = phase[:, b * 128 : (b + 1) * 128]
            return carry

        lax.fori_loop(0, SLOTS, slot_body, 0)
        for d in range(1, NZ):
            target = at_z(d)
            block = pl.ds(pl.multiple_of(target * SLOTS, SLOTS), SLOTS)
            mine_there = pl.ds(pl.multiple_of(z * SLOTS, SLOTS), SLOTS)
            send(ph.at[h, :, block], pa.at[h, :, mine_there], pa_s.at[h], pa_r.at[h], dev_z(d))
        here = pl.ds(pl.multiple_of(z * SLOTS, SLOTS), SLOTS)
        pa[h, :, here] = ph[h, :, here]

    for h in range(nc):
        columns = pl.ds(h * width, width)
        for k in range(NREF):
            total = None
            for j in range(LOOKS):
                a, b = rf[h, j, k], rf[h, LOOKS + j, k]
                term = a * a + b * b
                total = term if j == 0 else total + term
            quant[2 * SLOTS + k, :, columns] = total

        def power_body(s, carry, h=h, columns=columns):
            total = None
            for j in range(LOOKS):
                c, d = xg[lax.rem(s, A_DEV), s // A_DEV, h, 0, j], xg[lax.rem(s, A_DEV), s // A_DEV, h, 1, j]
                term = c * c + d * d
                total = term if j == 0 else total + term
            quant[2 * SLOTS + NREF + s, :, columns] = total
            return carry

        lax.fori_loop(0, ACQS, power_body, 0)

    col = lax.broadcasted_iota(jnp.int32, (ROWS, COLS), 1)
    row = lax.broadcasted_iota(jnp.int32, (ROWS, COLS), 0)

    def moved(v, by):
        out = pltpu.roll(v, by % COLS, 1)
        return jnp.where(col >= by, out, 0.0) if by > 0 else jnp.where(col < COLS + by, out, 0.0)

    def column_body(q, carry):
        v = quant[q]
        v = v + moved(v, 1) + moved(v, 2) + moved(v, -1) + moved(v, -2)
        quant[q] = v
        hlo[pl.ds(q, 1), :] = v[0:1, :]
        hhi[pl.ds(q, 1), :] = v[ROWS - 1 : ROWS, :]
        return carry

    lax.fori_loop(0, QUANT, column_body, 0)
    for rest in (hlo, hhi):
        rest[QUANT:QPAD, :] = jnp.zeros((QPAD - QUANT, COLS), jnp.float32)
    send(hlo, rhi, h_s.at[0], h_r.at[0], dev_q(-1))
    send(hhi, rlo, h_s.at[1], h_r.at[1], dev_q(1))
    wait(rhi, h_r.at[0])
    wait(rlo, h_r.at[1])
    below = jnp.where(place > 0, 1.0, 0.0)
    above = jnp.where(place < 31, 1.0, 0.0)

    def boxed(q):
        v = quant[q]
        down = jnp.where(row == 0, rlo[pl.ds(q, 1), :] * below, pltpu.roll(v, 1, 0))
        up = jnp.where(row == ROWS - 1, rhi[pl.ds(q, 1), :] * above, pltpu.roll(v, ROWS - 1, 0))
        return v + down + up

    def power_box(q, carry):
        quant[2 * SLOTS + q] = boxed(2 * SLOTS + q)
        return carry

    lax.fori_loop(0, NREF + ACQS, power_box, 0)

    def coherence_body(s, carry):
        group, index = s // CAP, lax.rem(s, CAP)
        kind, spot, live = info_s[group, index, 0], info_s[group, index, 1], info_s[group, index, 2]
        real, imag = boxed(s), boxed(SLOTS + s)
        first = quant[2 * SLOTS + kind]
        second = quant[2 * SLOTS + NREF + group * A_DEV + spot]
        value = jnp.sqrt(real * real + imag * imag) / jnp.sqrt(first * second)
        coh[group, index] = jnp.where(live > 0, value, 0.0)
        return carry

    lax.fori_loop(0, SLOTS, coherence_body, 0)
    quarter = pl.ds(pl.multiple_of(x * ROWS, ROWS), ROWS)
    for d in range(1, NX):
        send(coh.at[at_x(d)], coherence.at[:, quarter, :], co_s, co_r, dev_x(d))
    coherence[:, quarter, :] = coh[x]

    for h in range(nc):
        wait(pa.at[h, :, pl.ds(0, (NZ - 1) * SLOTS)], pa_r.at[h])
        for b in range(BLOCKS // nc):
            series[pl.ds(h * width + b * 128, 128), :] = dot(pa[h, b], xt[...], ((0,), (0,)))

    wait(coh.at[three], co_r)
    wait(coh.at[three], co_s)
    wait(info.at[three], is_)
    wait(da.at[0, three], d2s.at[0])
    wait(da.at[seven], d2s.at[1])
    for c in range(A_DEV):
        wait(ps.at[c, three], s1s.at[c])
    for h in range(nc):
        wait(zs.at[h, seven], rs_s.at[h])
        wait(pa.at[h, :, pl.ds(0, (NZ - 1) * SLOTS)], pa_s.at[h])
        for way in range(2):
            for step in range(3):
                wait(rf.at[h, 0], ag_s.at[h, way, step])
            wait(rf.at[h, 0, low], ag_s.at[h, way, 3])
    wait(hlo, h_s.at[0])
    wait(hhi, h_s.at[1])


def call(chunks, nc, cid, stack, pairs, order, refs, owners):
    width = COLS // nc
    f32 = jnp.float32
    dma = pltpu.SemaphoreType.DMA
    smem = pl.BlockSpec(memory_space=pltpu.SMEM)
    vmem = pl.BlockSpec(memory_space=pltpu.VMEM)
    return pl.pallas_call(
        functools.partial(kernel, chunks, nc),
        out_shape=(
            jax.ShapeDtypeStruct((COLS, NACQ), f32),
            jax.ShapeDtypeStruct((CAP, NX * ROWS, COLS), f32),
        ),
        in_specs=[pl.BlockSpec(memory_space=pl.ANY), smem, smem, smem, smem],
        out_specs=(vmem, vmem),
        scratch_shapes=[
            pltpu.VMEM((A_DEV, BLOCKS, 2, NX * ROWS * LOOKS, 128), f32),
            pltpu.VMEM((A_DEV, NX, nc, 2, LOOKS, ROWS, width), f32),
            pltpu.VMEM((chunks, NX, nc, 2, LOOKS, ROWS, width), f32),
            pltpu.VMEM((A_DEV, NX, nc, 2, LOOKS, ROWS, width), f32),
            pltpu.VMEM((nc, NZ, NREF, ROWS, width), f32),
            pltpu.VMEM((nc, NZ, NREF, ROWS, width), f32),
            pltpu.VMEM((nc, NZ, NREF, ROWS, width), f32),
            pltpu.VMEM((nc, BLOCKS // nc, ROWS * SLOTS, 128), f32),
            pltpu.VMEM((nc, BLOCKS // nc, NZ * SLOTS, 128), f32),
            pltpu.VMEM((NX, CAP, 128), jnp.int32),
            pltpu.SMEM((NX, CAP, 128), jnp.int32),
            pltpu.VMEM((NZ, NX, CAP, NACQ), f32),
            pltpu.VMEM((NZ * NX * CAP, NACQ), f32),
            pltpu.VMEM((QUANT, ROWS, COLS), f32),
            pltpu.VMEM((QPAD, COLS), f32),
            pltpu.VMEM((QPAD, COLS), f32),
            pltpu.VMEM((QPAD, COLS), f32),
            pltpu.VMEM((QPAD, COLS), f32),
            pltpu.VMEM((NX, CAP, ROWS, COLS), f32),
            dma((A_DEV, BLOCKS)), dma((A_DEV,)), dma((A_DEV,)), dma, dma, dma, dma((2,)), dma((2,)),
            dma((nc,)), dma((nc,)), dma((nc, 2, 4)), dma((nc, 2, 4)), dma((nc,)), dma((nc,)),
            dma((2,)), dma((2,)), dma, dma, dma((A_DEV,)),
        ],
        compiler_params=pltpu.CompilerParams(
            collective_id=cid, has_side_effects=True, vmem_limit_bytes=48 << 20
        ),
        name=f"sbas{chunks}",
    )(stack, pairs, order, refs, owners)


def local(stack, pairs, order, refs):
    numbers = jnp.arange(NACQ, dtype=jnp.int32)
    slot = jnp.sum(jnp.where(order[None, :] == refs[:, None], numbers[None, :], 0), axis=1)
    owner = slot // A_DEV
    before = (owner[None, :] == owner[:, None]) & (slot[None, :] < slot[:, None])
    chunk = jnp.sum(before.astype(jnp.int32), axis=1)
    owners = jnp.concatenate([owner // NZ, owner % NZ, chunk]).astype(jnp.int32)
    crowd = jnp.max(chunk)
    variants = [functools.partial(call, 1, NC, 1), functools.partial(call, 2, NC, 2), functools.partial(call, 4, NC, 3)]
    pick = jnp.minimum(crowd, 2)
    return lax.switch(pick, variants, stack, pairs, order, refs, owners)


NC = 1


def solution(mesh):
    return jax.shard_map(
        local,
        mesh=mesh,
        in_specs=(P("acq", None, "tile", None), P("acq", None), P(), P()),
        out_specs=(P(("tile", "acq"), None), P("acq", "tile", None)),
        check_vma=False,
    )
```

time: 266 us -> 77.7 us (0.29)
  waiting for transfers between devices: 105 us -> 0 us
  Pallas kernels: 0 us -> 72.2 us
  other arithmetic: 58.6 us -> 1.78 us
  blocking collectives: 39.6 us -> 0 us
  between operations: 24.3 us -> 1.3 us
  local copies, waits for them, and re-layouts: 18.6 us -> 2.25 us
  starting transfers between devices: 15.7 us -> 0 us
  matrix products: 3 us -> 0 us
    psum x1 -> x0, waiting for transfers between devices: 102 us -> none  [broadcast(): return lax.psum(kept, axis)]
    pallas_call x0 -> x1, Pallas kernels: none -> 72.2 us  [call(): pl.pallas_call(functools.partial(kernel, chunks, nc), out_shape=(jax.Shap...]
    all_gather x1 -> x0, blocking collectives: 39.6 us -> none  [local(): all_pairs = lax.all_gather(pair_list, 'acq', axis=0, tiled=True)]
    another operation x7 -> x0, other arithmetic: 26.1 us -> none  [the longest x3 12.4 us: local(): factor = jnp.linalg.cholesky(normal)]
    select_n x5 -> x2, other arithmetic: 12.6 us -> 0.03 us  [local(): owners = jnp.concatenate([owner // NZ, owner % NZ, chunk]).astype(jnp.int32)]
    ppermute x2 -> x0, starting transfers between devices: 9.68 us -> none  [the longest x1 7.58 us: with_halo(): lax.ppermute(lax.slice_in_dim(block, block.shape[dim] - width, None, axis...]
    reduce_sum x6 -> x2, other arithmetic: 9.5 us -> 1.04 us  [the longest x1 0.85 us: local(): jnp.sum(jnp.where(order[None, :] == refs[:, None], numbers[None, :], 0),...]
    add x3 -> x0, other arithmetic: 7.88 us -> none  [the longest x1 4.79 us: local(): look_real = multilook(first_real * second_real + first_imag * second_imag)]
  transfers between devices with their start and end apart: 4 -> 0, of which waited for: 2 -> 0; matrix products, arithmetic and copies ran while one was open for 13% -> 0% of each run, Pallas kernels for 0% -> 0%
where the time goes in v1:
time: 77.7 us; the launch traced here: 77.5 us
  Pallas kernels  72.2 us (93%)
  local copies, waits for them, and re-layouts  2.25 us (3%)
  other arithmetic  1.78 us (2%)
  between operations  1.3 us (2%)
    pallas_call x1, Pallas kernels, call(): pl.pallas_call(functools.partial(kernel, chunks, nc), out_shape=(jax.Shap...  72.2 us

profile of v1, /device:TPU:1, one launch (start us, length us, event | category | flops | bytes accessed | tf_op | source)
XLA Modules:
  0.0 77.5 jit_solution(17560884711374766388)
XLA Ops:
  0.6 0.9 %select_reduce_fusion = s32[4]{0:T(128)S(1)} fusion(s32[128]{0:T(128)} %param.9, s32[4]{0:T(128)} %param.10), kind=kLoop, calls=%fused_computation.1 | loop fusion | flops 1532 | bytes 544 | tf_op jit(solution)/shard_map/reduce_sum | solution.py:452
  1.5 0.2 convert_reduce_fusion
  1.7 0.6 reduce_max.9
  3.0 0.1 pad_add_fusion
  3.1 73.0 %conditional.1 = ((f32[512,128]{1,0:T(8,128)S(1)}, f32[8,32,512]{2,1,0:T(8,128)S(1)})) conditional(s32[]{:T(128)} %clamp.3, (f32[4,2,128,512]{3,2,1,0:T(8,128)}, s32[8,2]{0,1:T(2,128)}, s32[128]{0:T(128)}, s32[4]{0:T(128)}, s32[12]{0:T(128)S(1)}) %tuple.16, (f32[4,2,128,512]{3,2,1,0:T(8,128)}, s32[8,2]{0,1:T(2,128)}, s32[128]{0:T(128)}, ...), branch_computations={%region_3.4_spmd, %region_4.5_spmd, %region_5.6_spmd} | conditional | bytes 136 | solution.py:460
  3.1 0.8 copy.21.pairs
  3.8 72.2 %sbas1.1 = (f32[512,128]{1,0:T(8,128)S(1)}, f32[8,32,512]{2,1,0:T(8,128)S(1)}) custom-call(f32[4,2,128,512]{3,2,1,0:T(8,128)} %get-tuple-element.61.stack_hbm, s32[8,2]{1,0:T(8,128)S(1)} %copy.21.pairs, s32[128]{0:T(128)} %get-tuple-element.32.order, s32[4]{0:T(128)} %get-tuple-element.33.refs, s32[12]{0:T(128)S(1)} %get-tuple-element.34.owners), custom_call_target="tpu_custom_call" | custom-call | tf_op jit(solution)/shard_map/cond/branch_0_fun/sbas1/pallas_call | solution.py:411
  76.0 0.7 copy.32
  76.8 0.8 %copy.33 = f32[8,32,512]{2,1,0:T(8,128)} copy(f32[8,32,512]{2,1,0:T(8,128)S(1)} %get-tuple-element.108) | data formatting | bytes 1048576
  (2 shorter events, 0.0 us)

commit v2 on v1

v2 whole, which is shorter than its diff:
```python
import functools

import jax
import jax.numpy as jnp
from jax import lax
from jax.experimental import pallas as pl
from jax.experimental.pallas import tpu as pltpu
from jax.sharding import PartitionSpec as P

MESH = pl.DeviceIdType.MESH
HIGHEST = lax.Precision.HIGHEST
NREF = 4
LOOKS = 4
NX = 4
NZ = 8
A_DEV = 4
CAP = 8
COLS = 512
BLOCKS = 4
ROWS = 8
NACQ = 128
SLOTS = NX * CAP
ACQS = NX * A_DEV
QUANT = 2 * SLOTS + NREF + ACQS
QPAD = 88

ATAN = (
    1.0, -0.33333277702331543, 0.1999807506799698, -0.1426001638174057, 0.1093234121799469,
    -0.08349724858999252, 0.05708955600857735, -0.03035186603665352, 0.010487649589776993,
    -0.0017011701129376888,
)


def atan2(y, x):
    ax, ay = jnp.abs(x), jnp.abs(y)
    t = jnp.minimum(ax, ay) / jnp.maximum(ax, ay)
    u = t * t
    acc = jnp.full_like(u, ATAN[-1])
    for coefficient in ATAN[-2::-1]:
        acc = acc * u + coefficient
    r = acc * t
    r = jnp.where(ay > ax, jnp.pi / 2 - r, r)
    r = jnp.where(x < 0, jnp.pi - r, r)
    return jnp.where(y < 0, -r, r)


def dot(a, b, dims):
    return lax.dot_general(a, b, (dims, ((), ())), precision=HIGHEST, preferred_element_type=jnp.float32)


def make_solver(design, refs):
    lane = lax.broadcasted_iota(jnp.int32, (8, NACQ), 1)
    sub = lax.broadcasted_iota(jnp.int32, (8, NACQ), 0)
    pick = jnp.zeros((8, NACQ), jnp.float32)
    for k in range(NREF):
        pick = jnp.where((sub == k) & (lane == refs[k]), 1.0, pick)
    is_ref = jnp.sum(pick, axis=0, keepdims=True)
    other = 1.0 - is_ref
    degree = jnp.sum(design * design, axis=0, keepdims=True)
    inverse = other / (1.0 + degree)
    on_ref = dot(design, pick, ((1,), (1,)))
    normal_ref = dot(on_ref, design, ((0,), (0,))) + pick
    right = on_ref - dot(design * inverse, normal_ref, ((1,), (1,)))
    schur = dot(normal_ref, pick, ((1,), (1,))) - dot(normal_ref * inverse, normal_ref, ((1,), (1,)))
    row8 = lax.broadcasted_iota(jnp.int32, (8, 8), 0)
    col8 = lax.broadcasted_iota(jnp.int32, (8, 8), 1)
    eye8 = jnp.where(row8 == col8, 1.0, 0.0)
    left = schur + jnp.where(row8 >= NREF, eye8, 0.0)
    inv = eye8
    for k in range(NREF):
        pivot = 1.0 / left[k : k + 1, k : k + 1]
        lrow, irow = left[k : k + 1, :] * pivot, inv[k : k + 1, :] * pivot
        column = jnp.where(row8[:, 0:1] == k, 0.0, left[:, k : k + 1])
        left = jnp.where(row8 == k, lrow, left - column * lrow)
        inv = jnp.where(row8 == k, irow, inv - column * irow)
    at_ref = dot(right, inv, ((1,), (0,)))
    rest = (design - dot(at_ref, normal_ref, ((1,), (0,)))) * inverse
    return rest + dot(at_ref, pick, ((1,), (0,)))


def kernel(
    chunks, nc,
    stack_hbm, pairs, order, refs, series, coherence,
    stack, ps, xg, zs, zr, yx, yr, rf, ph, pa, info, info_s, da, xt, quant, hlo, hhi, rlo, rhi, coh,
    load_sem, s1s, s1r, i_sem, is_, ir, d2s, d2r, rs_s, rs_r, y_s, y_r, ag_s, ag_r, pa_s, pa_r, h_s, h_r, co_s, co_r, own_sem,
):
    width = COLS // nc
    tile, acq = lax.axis_index("tile"), lax.axis_index("acq")
    x, z = acq // NZ, lax.rem(acq, NZ)

    def at_x(d):
        return lax.rem(x + d, NX)

    def at_z(d):
        return lax.rem(z + d, NZ)

    def dev_x(d):
        return (tile, at_x(d) * NZ + z)

    def dev_z(d):
        return (tile, x * NZ + at_z(d))

    place = tile * NX + x

    def dev_q(d):
        q = lax.rem(place + d + 32, 32)
        return (q // NX, lax.rem(q, NX) * NZ + z)

    loads = []
    for a in range(A_DEV):
        for b in range(BLOCKS):
            copy = pltpu.make_async_copy(
                stack_hbm.at[a, :, :, pl.ds(b * 128, 128)], stack.at[a, b], load_sem.at[a, b]
            )
            copy.start()
            loads.append(copy)

    barrier = pltpu.get_barrier_semaphore()
    partners = [dev_x(d) for d in range(1, NX)] + [dev_z(d) for d in range(1, NZ)] + [dev_q(1), dev_q(-1)]
    for partner in partners:
        pl.semaphore_signal(barrier, inc=1, device_id=partner, device_id_type=MESH)

    def send(src, dst, ssem, rsem, device):
        copy = pltpu.make_async_remote_copy(
            src_ref=src, dst_ref=dst, send_sem=ssem, recv_sem=rsem, device_id=device, device_id_type=MESH
        )
        copy.start()

    def wait(ref, sem):
        pltpu.make_async_copy(ref, ref, sem).wait()

    mine = [order[acq * A_DEV + a] for a in range(A_DEV)]
    ref_no = [refs[k] for k in range(NREF)]
    is_ref = []
    for a in range(A_DEV):
        hit = jnp.int32(0)
        for k in range(NREF):
            hit = hit + jnp.where(mine[a] == ref_no[k], 1, 0)
        is_ref.append(jnp.minimum(hit, 1))
    n_ref = is_ref[0] + is_ref[1] + is_ref[2] + is_ref[3]
    position, refs_before, others_before = [], jnp.int32(0), jnp.int32(0)
    for a in range(A_DEV):
        position.append(jnp.where(is_ref[a] > 0, refs_before, n_ref + others_before))
        refs_before = refs_before + is_ref[a]
        others_before = others_before + 1 - is_ref[a]
    local = []
    for c in range(A_DEV):
        where = jnp.int32(0)
        for a in range(A_DEV):
            where = where + jnp.where(position[a] == c, a, 0)
        local.append(jnp.minimum(where, A_DEV - 1))

    lane = lax.broadcasted_iota(jnp.int32, (CAP, 128), 1)
    sub = lax.broadcasted_iota(jnp.int32, (CAP, 128), 0)
    rows = jnp.zeros((CAP, 128), jnp.float32)
    facts = jnp.zeros((CAP, 128), jnp.int32)
    for s in range(CAP):
        kind, second = pairs[s, 0], pairs[s, 1]
        live = jnp.where(kind >= 0, 1, 0)
        kind = jnp.maximum(kind, 0)
        first = refs[kind]
        spot = jnp.int32(0)
        for a in range(A_DEV):
            spot = spot + jnp.where(mine[a] == second, a, 0)
        spot = jnp.minimum(spot, A_DEV - 1)
        row = jnp.where(lane == first, 1.0, 0.0) - jnp.where(lane == second, 1.0, 0.0)
        row = jnp.where(live > 0, row, 0.0)
        rows = jnp.where(sub == s, row, rows)
        fact = jnp.where(lane == 0, kind, jnp.where(lane == 1, spot, jnp.where(lane == 2, live, 0)))
        facts = jnp.where(sub == s, fact, facts)
    info[x] = facts
    da[z, x] = rows

    for copy in loads:
        copy.wait()

    def arrange(c):
        def body(t, carry):
            q, part = t // 2, lax.rem(t, 2)
            for j in range(LOOKS):
                for b in range(BLOCKS):
                    h, inner = divmod(b, BLOCKS // nc)
                    ps[c, q, h, part, j, :, pl.ds(inner * 128, 128)] = stack[
                        c, b, part, pl.ds(q * (ROWS * LOOKS) + j, ROWS, stride=LOOKS), :
                    ]
            return carry

        lax.fori_loop(0, NX * 2, body, 0)

    own = {}
    three, seven = pl.ds(0, NX - 1), pl.ds(0, NZ - 1)

    def send_chunk(c, h):
        for d in (1, 3, 2):
            send(ps.at[c, at_x(d), h], xg[h].at[c, x], s1s.at[c, h], s1r.at[c, h], dev_x(d))
        own[c, h] = pltpu.make_async_copy(ps.at[c, x, h], xg[h].at[c, x], own_sem.at[c, h])
        own[c, h].start()

    def sent(c, h):
        wait(ps.at[c, three, h], s1s.at[c, h])

    def arrived(c, h):
        wait(xg[h].at[c, three], s1r.at[c, h])
        own[c, h].wait()

    def scatter_fill():
        for r in range(chunks):
            def body(q, carry, r=r):
                for part in range(2):
                    for j in range(LOOKS):
                        for b in range(BLOCKS):
                            zs[part * LOOKS + j, r, q, :, pl.ds(b * 128, 128)] = stack[
                                local[r], b, part, pl.ds(q * (ROWS * LOOKS) + j, ROWS, stride=LOOKS), :
                            ]
                return carry

            lax.fori_loop(0, NX, body, 0)

    def scatter():
        for d in (4, 3, 5, 2, 6, 1, 7):
            send(zs.at[at_z(d)], zr.at[z], rs_s, rs_r, dev_z(d))
        zr[z] = zs[z]

    def find(n, slots):
        return tuple(slots[k] + jnp.where(order[n] == ref_no[k], n, 0) for k in range(NREF))

    def scatter_x(where_ref):
        wait(zr.at[seven], rs_r)
        for k in range(NREF):
            _, rz, rank = where_ref[k]
            for q in range(NX):
                yx[q, k] = zr[rz, rank, q]
        for d in (2, 1, 3):
            send(yx.at[at_x(d)], yr.at[x], y_s, y_r, dev_x(d))
        yr[x] = yx[x]

    half = NREF // 2
    halves = (pl.ds(0, half), pl.ds(half, half))

    def sign(way, d):
        return d if way == 0 else NZ - d

    def gather_first(h, where_ref):
        wait(yr.at[three], y_r)
        for k in range(NREF):
            rf[h][z, k] = yr[where_ref[k][0], k]
        for d in (2, 1):
            for way in range(2):
                send(
                    rf[h].at[z], rf[h].at[z], ag_s.at[h, way, d - 1], ag_r.at[h, way, d - 1], dev_z(sign(way, d))
                )

    def gather_second(h):
        for way in range(2):
            origin = at_z(sign(way, NZ - 2))
            wait(rf[h].at[origin], ag_r.at[h, way, 1])
            send(rf[h].at[origin], rf[h].at[origin], ag_s.at[h, way, 2], ag_r.at[h, way, 2], dev_z(sign(way, 1)))
            part = rf[h].at[origin, halves[way]]
            send(part, part, ag_s.at[h, way, 3], ag_r.at[h, way, 3], dev_z(sign(way, 2)))

    def gathered(h):
        for way in range(2):
            wait(rf[h].at[0], ag_r.at[h, way, 0])
            wait(rf[h].at[0], ag_r.at[h, way, 2])
            wait(rf[h].at[0, halves[way]], ag_r.at[h, way, 3])

    def solve():
        wait(da.at[seven], d2r.at[1])
        xt[...] = make_solver(da[...].reshape(NZ * NX * CAP, NACQ), ref_no)

    def facts_around():
        wait(info.at[three], ir)
        to_smem = pltpu.make_async_copy(info, info_s, i_sem)
        to_smem.start()
        wait(da.at[0, three], d2r.at[0])
        for d in range(1, NZ):
            send(da.at[z], da.at[z], d2s.at[1], d2r.at[1], dev_z(d))
        to_smem.wait()

    scatter_fill()
    pl.semaphore_wait(barrier, len(partners))
    scatter()
    for d in range(1, NX):
        send(info.at[x], info.at[x], is_, ir, dev_x(d))
        send(da.at[z, x], da.at[z, x], d2s.at[0], d2r.at[0], dev_x(d))
    for c in range(2):
        arrange(c)
        send_chunk(c, 0)
    for c in range(2, A_DEV):
        arrange(c)
    slots = lax.fori_loop(0, NACQ, find, (jnp.int32(0),) * NREF)
    slots = [jnp.minimum(slot, NACQ - 1) for slot in slots]
    owner = [lax.shift_right_logical(slot, 2) for slot in slots]
    where_ref = []
    for k in range(NREF):
        rank = jnp.int32(0)
        for other in range(NREF):
            if other != k:
                rank = rank + jnp.where((owner[other] == owner[k]) & (slots[other] < slots[k]), 1, 0)
        where_ref.append(
            (lax.shift_right_logical(owner[k], 3), lax.rem(owner[k], NZ), jnp.minimum(rank, chunks - 1))
        )
    facts_around()
    scatter_x(where_ref)
    wait(yx.at[three], y_s)
    for c in range(2, A_DEV):
        send_chunk(c, 0)
    gather_first(0, where_ref)
    gather_second(0)
    solve()

    def keep(q, v, columns):
        quant[q, :, columns] = v
        hlo[pl.ds(q, 1), columns] = v[0:1, :]
        hhi[pl.ds(q, 1), columns] = v[ROWS - 1 : ROWS, :]

    def powers(h):
        columns = pl.ds(h * width, width)
        for k in range(NREF):
            total = None
            for j in range(LOOKS):
                a, b = rf[h][j, k], rf[h][LOOKS + j, k]
                term = a * a + b * b
                total = term if j == 0 else total + term
            keep(2 * SLOTS + k, total, columns)

        def power_body(s, carry):
            total = None
            for j in range(LOOKS):
                c, d = xg[h][lax.rem(s, A_DEV), s // A_DEV, 0, j], xg[h][lax.rem(s, A_DEV), s // A_DEV, 1, j]
                term = c * c + d * d
                total = term if j == 0 else total + term
            keep(2 * SLOTS + NREF + s, total, columns)
            return carry

        lax.fori_loop(0, ACQS, power_body, 0)

    def interferograms(h):
        gathered(h)
        for c in range(A_DEV):
            arrived(c, h)
        powers(h)
        columns = pl.ds(h * width, width)

        def slot_body(s, carry):
            group, index = s // CAP, lax.rem(s, CAP)
            kind, spot, live = info_s[group, index, 0], info_s[group, index, 1], info_s[group, index, 2]
            real = imag = None
            for j in range(LOOKS):
                a, b = rf[h][j, kind], rf[h][LOOKS + j, kind]
                c, d = xg[h][spot, group, 0, j], xg[h][spot, group, 1, j]
                re, im = a * c + b * d, b * c - a * d
                real, imag = (re, im) if j == 0 else (real + re, imag + im)
            for q, v in ((s, real), (SLOTS + s, imag)):
                keep(q, v, columns)
            phase = jnp.where(live > 0, atan2(imag, real), 0.0)
            for b in range(BLOCKS // nc):
                ph[h, b, pl.ds(s, ROWS, stride=SLOTS), :] = phase[:, b * 128 : (b + 1) * 128]
            return carry

        lax.fori_loop(0, SLOTS, slot_body, 0)
        for rest in (hlo, hhi):
            rest[QUANT:QPAD, columns] = jnp.zeros((QPAD - QUANT, width), jnp.float32)
        send(hlo.at[:, columns], rhi.at[:, columns], h_s.at[0, h], h_r.at[0, h], dev_q(-1))
        send(hhi.at[:, columns], rlo.at[:, columns], h_s.at[1, h], h_r.at[1, h], dev_q(1))
        for d in range(1, NZ):
            target = at_z(d)
            block = pl.ds(pl.multiple_of(target * SLOTS, SLOTS), SLOTS)
            mine_there = pl.ds(pl.multiple_of(z * SLOTS, SLOTS), SLOTS)
            send(ph.at[h, :, block], pa.at[h, :, mine_there], pa_s.at[h], pa_r.at[h], dev_z(d))
        here = pl.ds(pl.multiple_of(z * SLOTS, SLOTS), SLOTS)
        pa[h, :, here] = ph[h, :, here]

    for h in range(nc):
        interferograms(h)

    col = lax.broadcasted_iota(jnp.int32, (ROWS, COLS), 1)
    row = lax.broadcasted_iota(jnp.int32, (ROWS, COLS), 0)

    def five(v):
        out = v
        for by in (1, 2):
            out = out + jnp.where(col >= by, pltpu.roll(v, by, 1), 0.0)
            out = out + jnp.where(col < COLS - by, pltpu.roll(v, COLS - by, 1), 0.0)
        return out

    def column_body(t, carry):
        values = [five(quant[4 * t + i]) for i in range(4)]
        for i in range(4):
            quant[4 * t + i] = values[i]
        return carry

    lax.fori_loop(0, QUANT // 4, column_body, 0)
    for h in range(nc):
        columns = pl.ds(h * width, width)
        wait(rhi.at[:, columns], h_r.at[0, h])
        wait(rlo.at[:, columns], h_r.at[1, h])
    below = jnp.where(place > 0, 1.0, 0.0)
    above = jnp.where(place < 31, 1.0, 0.0)

    def halo_body(t, carry):
        block = pl.ds(pl.multiple_of(t * 8, 8), 8)
        lo, hi = five(rlo[block, :]) * below, five(rhi[block, :]) * above
        rlo[block, :], rhi[block, :] = lo, hi
        return carry

    lax.fori_loop(0, QPAD // 8, halo_body, 0)

    def boxed(q):
        v = quant[q]
        down = jnp.where(row == 0, rlo[pl.ds(q, 1), :], pltpu.roll(v, 1, 0))
        up = jnp.where(row == ROWS - 1, rhi[pl.ds(q, 1), :], pltpu.roll(v, ROWS - 1, 0))
        return v + down + up

    def power_box(t, carry):
        values = [boxed(2 * SLOTS + 4 * t + i) for i in range(4)]
        for i in range(4):
            quant[2 * SLOTS + 4 * t + i] = values[i]
        return carry

    lax.fori_loop(0, (NREF + ACQS) // 4, power_box, 0)
    quarter = pl.ds(pl.multiple_of(x * ROWS, ROWS), ROWS)
    for d in (2, 1, 3, 0):
        group = at_x(d)

        def coherence_body(t, carry, group=group):
            values = []
            for i in range(2):
                index = 2 * t + i
                s = group * CAP + index
                kind, spot, live = info_s[group, index, 0], info_s[group, index, 1], info_s[group, index, 2]
                real, imag = boxed(s), boxed(SLOTS + s)
                first = quant[2 * SLOTS + kind]
                second = quant[2 * SLOTS + NREF + group * A_DEV + spot]
                value = jnp.sqrt(real * real + imag * imag) / jnp.sqrt(first * second)
                values.append(jnp.where(live > 0, value, 0.0))
            for i in range(2):
                coh[group, 2 * t + i] = values[i]
            return carry

        lax.fori_loop(0, CAP // 2, coherence_body, 0)
        if d:
            send(coh.at[group], coherence.at[:, quarter, :], co_s, co_r, dev_x(d))
    coherence[:, quarter, :] = coh[x]

    for h in range(nc):
        wait(pa.at[h, :, pl.ds(0, (NZ - 1) * SLOTS)], pa_r.at[h])
        for b in range(BLOCKS // nc):
            series[pl.ds(h * width + b * 128, 128), :] = dot(pa[h, b], xt[...], ((0,), (0,)))

    wait(coh.at[three], co_r)
    wait(coh.at[three], co_s)
    wait(info.at[three], is_)
    wait(da.at[0, three], d2s.at[0])
    wait(da.at[seven], d2s.at[1])
    for h in range(nc):
        for c in range(A_DEV):
            sent(c, h)
        wait(zs.at[seven], rs_s)
        wait(pa.at[h, :, pl.ds(0, (NZ - 1) * SLOTS)], pa_s.at[h])
        for way in range(2):
            for step in range(3):
                wait(rf[h].at[0], ag_s.at[h, way, step])
            wait(rf[h].at[0, halves[way]], ag_s.at[h, way, 3])
        columns = pl.ds(h * width, width)
        wait(hlo.at[:, columns], h_s.at[0, h])
        wait(hhi.at[:, columns], h_s.at[1, h])


def call(chunks, nc, cid, stack, pairs, order, refs):
    width = COLS // nc
    f32 = jnp.float32
    dma = pltpu.SemaphoreType.DMA
    smem = pl.BlockSpec(memory_space=pltpu.SMEM)
    vmem = pl.BlockSpec(memory_space=pltpu.VMEM)
    return pl.pallas_call(
        functools.partial(kernel, chunks, nc),
        out_shape=(
            jax.ShapeDtypeStruct((COLS, NACQ), f32),
            jax.ShapeDtypeStruct((CAP, NX * ROWS, COLS), f32),
        ),
        in_specs=[pl.BlockSpec(memory_space=pl.ANY), smem, smem, smem],
        out_specs=(vmem, vmem),
        scratch_shapes=[
            pltpu.VMEM((A_DEV, BLOCKS, 2, NX * ROWS * LOOKS, 128), f32),
            pltpu.VMEM((A_DEV, NX, nc, 2, LOOKS, ROWS, width), f32),
            [pltpu.VMEM((A_DEV, NX, 2, LOOKS, ROWS, width), f32)] * nc,
            pltpu.VMEM((NZ, chunks, NX, ROWS, COLS), f32),
            pltpu.VMEM((NZ, chunks, NX, ROWS, COLS), f32),
            pltpu.VMEM((NX, NREF, ROWS, COLS), f32),
            pltpu.VMEM((NX, NREF, ROWS, COLS), f32),
            [pltpu.VMEM((NZ, NREF, ROWS, width), f32)] * nc,
            pltpu.VMEM((nc, BLOCKS // nc, ROWS * SLOTS, 128), f32),
            pltpu.VMEM((nc, BLOCKS // nc, NZ * SLOTS, 128), f32),
            pltpu.VMEM((NX, CAP, 128), jnp.int32),
            pltpu.SMEM((NX, CAP, 128), jnp.int32),
            pltpu.VMEM((NZ, NX, CAP, NACQ), f32),
            pltpu.VMEM((NZ * NX * CAP, NACQ), f32),
            pltpu.VMEM((QUANT, ROWS, COLS), f32),
            pltpu.VMEM((QPAD, COLS), f32),
            pltpu.VMEM((QPAD, COLS), f32),
            pltpu.VMEM((QPAD, COLS), f32),
            pltpu.VMEM((QPAD, COLS), f32),
            pltpu.VMEM((NX, CAP, ROWS, COLS), f32),
            dma((A_DEV, BLOCKS)), dma((A_DEV, nc)), dma((A_DEV, nc)), dma, dma, dma, dma((2,)), dma((2,)),
            dma, dma, dma, dma, dma((nc, 2, 4)), dma((nc, 2, 4)), dma((nc,)), dma((nc,)),
            dma((2, nc)), dma((2, nc)), dma, dma, dma((A_DEV, nc)),
        ],
        compiler_params=pltpu.CompilerParams(
            collective_id=cid, has_side_effects=True, vmem_limit_bytes=48 << 20
        ),
        name=f"sbas{chunks}",
    )(stack, pairs, order, refs)


def local(stack, pairs, order, refs):
    numbers = lax.broadcasted_iota(jnp.int32, (NACQ, NACQ), 0) // A_DEV
    across = lax.broadcasted_iota(jnp.int32, (NACQ, NACQ), 1) // A_DEV
    rows = lax.broadcast_in_dim(order, (NACQ, NACQ), (0,))
    columns = lax.broadcast_in_dim(order, (NACQ, NACQ), (1,))
    one = [refs[k] for k in range(NREF)]
    held = (rows == one[0]) | (rows == one[1]) | (rows == one[2]) | (rows == one[3])
    also = (columns == one[0]) | (columns == one[1]) | (columns == one[2]) | (columns == one[3])
    together = jnp.sum((held & also & (numbers == across)).astype(jnp.int32))
    pick = jnp.where(together > 8, 2, jnp.where(together > 4, 1, 0))
    variants = [functools.partial(call, 1, NC, 1), functools.partial(call, 2, NC, 2), functools.partial(call, 4, NC, 3)]
    return lax.switch(pick, variants, stack, pairs, order, refs)


NC = 1


def solution(mesh):
    return jax.shard_map(
        local,
        mesh=mesh,
        in_specs=(P("acq", None, "tile", None), P("acq", None), P(), P()),
        out_specs=(P(("tile", "acq"), None), P("acq", "tile", None)),
        check_vma=False,
    )
```

time: 77.7 us -> 65.5 us (0.84)
  Pallas kernels: 72.2 us -> 55.5 us
  other arithmetic: 1.78 us -> 3.95 us
  local copies, waits for them, and re-layouts: 2.25 us -> 3.68 us
    pallas_call x1, Pallas kernels: 72.2 us -> 55.5 us  [call(): pl.pallas_call(functools.partial(kernel, chunks, nc), out_shape=(jax.Shap...]
    and x0 -> x1, other arithmetic: none -> 3.18 us  [local(): numbers = lax.broadcasted_iota(jnp.int32, (NACQ, NACQ), 0) // A_DEV]
    slice x0 -> x1, local copies, waits for them, and re-layouts: none -> 1.43 us  [local(): one = [refs[k] for k in range(NREF)]]
where the time goes in v2:
time: 65.5 us; the launch traced here: 65.1 us
  Pallas kernels  55.5 us (85%)
  other arithmetic  3.95 us (6%)
  local copies, waits for them, and re-layouts  3.68 us (6%)
  between operations  1.95 us (3%)
    pallas_call x1, Pallas kernels, call(): pl.pallas_call(functools.partial(kernel, chunks, nc), out_shape=(jax.Shap...  55.5 us
    and x1, other arithmetic, local(): numbers = lax.broadcasted_iota(jnp.int32, (NACQ, NACQ), 0) // A_DEV  3.18 us
    unnamed x2, local copies, waits for them, and re-layouts  1.5 us
    slice x1, local copies, waits for them, and re-layouts, local(): one = [refs[k] for k in range(NREF)]  1.43 us

profile of v2, /device:TPU:1, one launch (start us, length us, event | category | flops | bytes accessed | tf_op | source)
XLA Modules:
  0.0 65.1 jit_solution(16406491459152794274)
XLA Ops:
  0.6 1.4 %fusion.1 = (s32[1]{0:T(128)}, s32[1]{0:T(128)}, s32[1]{0:T(128)}, s32[1]{0:T(128)}) fusion(s32[4]{0:T(128)} %param.10), kind=kLoop, calls=%fused_computation.9 | loop fusion | bytes 32 | tf_op jit(solution)/shard_map/slice | solution.py:521
  2.1 3.2 %compare_and_fusion = (pred[128]{0:T(512)(128)(4,1)S(1)}, pred[128]{0:T(512)(128)(4,1)S(1)}) fusion(s32[128]{0:T(128)} %param.9, s32[]{:T(128)} %bitcast.3, s32[]{:T(128)} %bitcast.2, s32[]{:T(128)} %bitcast.1, s32[]{:T(128)} %bitcast), kind=kLoop, calls=%fused_computation.3 | loop fusion | flops 1536 | bytes 784 | tf_op jit(solution)/shard_map/jit(floor_divide)/and | solution.py:517
  5.2 0.8 %convert_reduce_fusion = s32[]{:T(128)} fusion(s32[128]{0:T(128)S(1)} %get-tuple-element.76, s32[128]{0:T(128)S(1)} %get-tuple-element.77, pred[128]{0:T(512)(128)(4,1)S(1)} %get-tuple-element.74, pred[128]{0:T(512)(128)(4,1)S(1)} %get-tuple-element.75), kind=kLoop, calls=%fused_computation | loop fusion | flops 114687 | bytes 1284 | tf_op jit(solution)/shard_map/reduce_sum | solution.py:524
  7.3 56.3 %conditional.1 = ((f32[512,128]{1,0:T(8,128)S(1)}, f32[8,32,512]{2,1,0:T(8,128)S(1)})) conditional(s32[]{:T(128)} %clamp.3, (f32[4,2,128,512]{3,2,1,0:T(8,128)}, s32[8,2]{0,1:T(2,128)}, s32[128]{0:T(128)}, s32[4]{0:T(128)}) %tuple.16, (f32[4,2,128,512]{3,2,1,0:T(8,128)}, s32[8,2]{0,1:T(2,128)}, s32[128]{0:T(128)}, ...), branch_computations={%region_1.2_spmd, %region_2.3_spmd, %region_3.4_spmd} | conditional | bytes 136 | solution.py:527
  7.3 0.8 %copy.15.pairs = s32[8,2]{1,0:T(8,128)S(1)} copy(s32[8,2]{0,1:T(2,128)} %get-tuple-element.59) | data formatting | bytes 128 | tf_op jit(solution)/shard_map
  8.1 55.5 %sbas1.1 = (f32[512,128]{1,0:T(8,128)S(1)}, f32[8,32,512]{2,1,0:T(8,128)S(1)}) custom-call(f32[4,2,128,512]{3,2,1,0:T(8,128)} %get-tuple-element.24.stack_hbm, s32[8,2]{1,0:T(8,128)S(1)} %copy.15.pairs, s32[128]{0:T(128)} %get-tuple-element.26.order, s32[4]{0:T(128)} %get-tuple-element.27.refs), custom_call_target="tpu_custom_call" | custom-call | tf_op jit(solution)/shard_map/cond/branch_0_fun/sbas1/pallas_call | solution.py:476
  63.6 0.7 %copy.26 = f32[512,128]{1,0:T(8,128)} copy(f32[512,128]{1,0:T(8,128)S(1)} %get-tuple-element.86) | data formatting | bytes 524288
  64.3 0.8 %copy.27 = f32[8,32,512]{2,1,0:T(8,128)} copy(f32[8,32,512]{2,1,0:T(8,128)S(1)} %get-tuple-element.87) | data formatting | bytes 1048576
  (1 shorter events, 0.0 us)

commit v3 on v2

--- a/solution.py
+++ b/solution.py
@@ -155,7 +155,7 @@
     rows = jnp.zeros((CAP, 128), jnp.float32)
     facts = jnp.zeros((CAP, 128), jnp.int32)
     for s in range(CAP):
-        kind, second = pairs[s, 0], pairs[s, 1]
+        kind, second = pairs[0, s], pairs[1, s]
         live = jnp.where(kind >= 0, 1, 0)
         kind = jnp.maximum(kind, 0)
         first = refs[kind]
@@ -245,6 +245,9 @@
         for k in range(NREF):
             rf[h][z, k] = yr[where_ref[k][0], k]
         for d in (2, 1):
+            if d == 1:
+                for way in range(2):
+                    wait(rf[h].at[z], ag_s.at[h, way, 1])
             for way in range(2):
                 send(
                     rf[h].at[z], rf[h].at[z], ag_s.at[h, way, d - 1], ag_r.at[h, way, d - 1], dev_z(sign(way, d))
@@ -314,68 +317,12 @@
         hlo[pl.ds(q, 1), columns] = v[0:1, :]
         hhi[pl.ds(q, 1), columns] = v[ROWS - 1 : ROWS, :]
 
-    def powers(h):
-        columns = pl.ds(h * width, width)
-        for k in range(NREF):
-            total = None
-            for j in range(LOOKS):
-                a, b = rf[h][j, k], rf[h][LOOKS + j, k]
-                term = a * a + b * b
-                total = term if j == 0 else total + term
-            keep(2 * SLOTS + k, total, columns)
-
-        def power_body(s, carry):
-            total = None
-            for j in range(LOOKS):
-                c, d = xg[h][lax.rem(s, A_DEV), s // A_DEV, 0, j], xg[h][lax.rem(s, A_DEV), s // A_DEV, 1, j]
-                term = c * c + d * d
-                total = term if j == 0 else total + term
-            keep(2 * SLOTS + NREF + s, total, columns)
-            return carry
-
-        lax.fori_loop(0, ACQS, power_body, 0)
-
-    def interferograms(h):
-        gathered(h)
-        for c in range(A_DEV):
-            arrived(c, h)
-        powers(h)
-        columns = pl.ds(h * width, width)
-
-        def slot_body(s, carry):
-            group, index = s // CAP, lax.rem(s, CAP)
-            kind, spot, live = info_s[group, index, 0], info_s[group, index, 1], info_s[group, index, 2]
-            real = imag = None
-            for j in range(LOOKS):
-                a, b = rf[h][j, kind], rf[h][LOOKS + j, kind]
-                c, d = xg[h][spot, group, 0, j], xg[h][spot, group, 1, j]
-                re, im = a * c + b * d, b * c - a * d
-                real, imag = (re, im) if j == 0 else (real + re, imag + im)
-            for q, v in ((s, real), (SLOTS + s, imag)):
-                keep(q, v, columns)
-            phase = jnp.where(live > 0, atan2(imag, real), 0.0)
-            for b in range(BLOCKS // nc):
-                ph[h, b, pl.ds(s, ROWS, stride=SLOTS), :] = phase[:, b * 128 : (b + 1) * 128]
-            return carry
-
-        lax.fori_loop(0, SLOTS, slot_body, 0)
-        for rest in (hlo, hhi):
-            rest[QUANT:QPAD, columns] = jnp.zeros((QPAD - QUANT, width), jnp.float32)
-        send(hlo.at[:, columns], rhi.at[:, columns], h_s.at[0, h], h_r.at[0, h], dev_q(-1))
-        send(hhi.at[:, columns], rlo.at[:, columns], h_s.at[1, h], h_r.at[1, h], dev_q(1))
-        for d in range(1, NZ):
-            target = at_z(d)
-            block = pl.ds(pl.multiple_of(target * SLOTS, SLOTS), SLOTS)
-            mine_there = pl.ds(pl.multiple_of(z * SLOTS, SLOTS), SLOTS)
-            send(ph.at[h, :, block], pa.at[h, :, mine_there], pa_s.at[h], pa_r.at[h], dev_z(d))
-        here = pl.ds(pl.multiple_of(z * SLOTS, SLOTS), SLOTS)
-        pa[h, :, here] = ph[h, :, here]
-
-    for h in range(nc):
-        interferograms(h)
-
     col = lax.broadcasted_iota(jnp.int32, (ROWS, COLS), 1)
     row = lax.broadcasted_iota(jnp.int32, (ROWS, COLS), 0)
+    below = jnp.where(place > 0, 1.0, 0.0)
+    above = jnp.where(place < 31, 1.0, 0.0)
+    pairs_rows = 2 * CAP
+    power_rows = pl.ds(2 * SLOTS, QPAD - 2 * SLOTS)
 
     def five(v):
         out = v
@@ -384,27 +331,29 @@
             out = out + jnp.where(col < COLS - by, pltpu.roll(v, COLS - by, 1), 0.0)
         return out
 
-    def column_body(t, carry):
-        values = [five(quant[4 * t + i]) for i in range(4)]
-        for i in range(4):
-            quant[4 * t + i] = values[i]
-        return carry
-
-    lax.fori_loop(0, QUANT // 4, column_body, 0)
-    for h in range(nc):
-        columns = pl.ds(h * width, width)
-        wait(rhi.at[:, columns], h_r.at[0, h])
-        wait(rlo.at[:, columns], h_r.at[1, h])
-    below = jnp.where(place > 0, 1.0, 0.0)
-    above = jnp.where(place < 31, 1.0, 0.0)
-
-    def halo_body(t, carry):
-        block = pl.ds(pl.multiple_of(t * 8, 8), 8)
-        lo, hi = five(rlo[block, :]) * below, five(rhi[block, :]) * above
-        rlo[block, :], rhi[block, :] = lo, hi
-        return carry
-
-    lax.fori_loop(0, QPAD // 8, halo_body, 0)
+    def group_rows(group):
+        return pl.ds(group * pairs_rows, pairs_rows)
+
+    def send_halo(rows_, piece):
+        send(hlo.at[rows_], rhi.at[rows_], h_s.at[0, piece], h_r.at[0, piece], dev_q(-1))
+        send(hhi.at[rows_], rlo.at[rows_], h_s.at[1, piece], h_r.at[1, piece], dev_q(1))
+
+    def halo_here(rows_, piece, count):
+        wait(rhi.at[rows_], h_r.at[0, piece])
+        wait(rlo.at[rows_], h_r.at[1, piece])
+        for i in range(count // 8):
+            block = pl.ds(rows_.start + 8 * i, 8)
+            lo, hi = five(rlo[block, :]) * below, five(rhi[block, :]) * above
+            rlo[block, :], rhi[block, :] = lo, hi
+
+    def column_sums(start, count):
+        def body(t, carry):
+            values = [five(quant[start + 4 * t + i]) for i in range(4)]
+            for i in range(4):
+                quant[start + 4 * t + i] = values[i]
+            return carry
+
+        lax.fori_loop(0, count // 4, body, 0)
 
     def boxed(q):
         v = quant[q]
@@ -412,6 +361,62 @@
         up = jnp.where(row == ROWS - 1, rhi[pl.ds(q, 1), :], pltpu.roll(v, ROWS - 1, 0))
         return v + down + up
 
+    for rest in (hlo, hhi):
+        rest[QUANT:QPAD, :] = jnp.zeros((QPAD - QUANT, COLS), jnp.float32)
+    gathered(0)
+    for c in range(A_DEV):
+        arrived(c, 0)
+    full = pl.ds(0, COLS)
+    for k in range(NREF):
+        total = None
+        for j in range(LOOKS):
+            a, b = rf[0][j, k], rf[0][LOOKS + j, k]
+            term = a * a + b * b
+            total = term if j == 0 else total + term
+        keep(2 * SLOTS + k, total, full)
+
+    def power_body(s, carry):
+        total = None
+        for j in range(LOOKS):
+            c, d = xg[0][lax.rem(s, A_DEV), s // A_DEV, 0, j], xg[0][lax.rem(s, A_DEV), s // A_DEV, 1, j]
+            term = c * c + d * d
+            total = term if j == 0 else total + term
+        keep(2 * SLOTS + NREF + s, total, full)
+        return carry
+
+    order_d = (2, 1, 3, 0)
+    for group in range(NX):
+
+        def slot_body(index, carry, group=group):
+            kind, spot, live = info_s[group, index, 0], info_s[group, index, 1], info_s[group, index, 2]
+            real = imag = None
+            for j in range(LOOKS):
+                a, b = rf[0][j, kind], rf[0][LOOKS + j, kind]
+                c, e = xg[0][spot, group, 0, j], xg[0][spot, group, 1, j]
+                re, im = a * c + b * e, b * c - a * e
+                real, imag = (re, im) if j == 0 else (real + re, imag + im)
+            keep(group * pairs_rows + index, real, full)
+            keep(group * pairs_rows + CAP + index, imag, full)
+            phase = jnp.where(live > 0, atan2(imag, real), 0.0)
+            for b in range(BLOCKS):
+                ph[0, b, pl.ds(group * CAP + index, ROWS, stride=SLOTS), :] = phase[:, b * 128 : (b + 1) * 128]
+            return carry
+
+        lax.fori_loop(0, CAP, slot_body, 0)
+        send_halo(group_rows(group), group)
+    for d in range(1, NZ):
+        target = at_z(d)
+        block = pl.ds(pl.multiple_of(target * SLOTS, SLOTS), SLOTS)
+        mine_there = pl.ds(pl.multiple_of(z * SLOTS, SLOTS), SLOTS)
+        send(ph.at[0, :, block], pa.at[0, :, mine_there], pa_s.at[0], pa_r.at[0], dev_z(d))
+    here = pl.ds(pl.multiple_of(z * SLOTS, SLOTS), SLOTS)
+    pa[0, :, here] = ph[0, :, here]
+
+    lax.fori_loop(0, ACQS, power_body, 0)
+    send_halo(power_rows, NX)
+    column_sums(0, QUANT)
+    halo_here(power_rows, NX, QPAD - 2 * SLOTS)
+
     def power_box(t, carry):
         values = [boxed(2 * SLOTS + 4 * t + i) for i in range(4)]
         for i in range(4):
@@ -419,17 +424,18 @@
         return carry
 
     lax.fori_loop(0, (NREF + ACQS) // 4, power_box, 0)
+    for group in range(NX):
+        halo_here(group_rows(group), group, pairs_rows)
     quarter = pl.ds(pl.multiple_of(x * ROWS, ROWS), ROWS)
-    for d in (2, 1, 3, 0):
+    for d in order_d:
         group = at_x(d)
 
         def coherence_body(t, carry, group=group):
             values = []
             for i in range(2):
                 index = 2 * t + i
-                s = group * CAP + index
                 kind, spot, live = info_s[group, index, 0], info_s[group, index, 1], info_s[group, index, 2]
-                real, imag = boxed(s), boxed(SLOTS + s)
+                real, imag = boxed(group * pairs_rows + index), boxed(group * pairs_rows + CAP + index)
                 first = quant[2 * SLOTS + kind]
                 second = quant[2 * SLOTS + NREF + group * A_DEV + spot]
                 value = jnp.sqrt(real * real + imag * imag) / jnp.sqrt(first * second)
@@ -459,12 +465,13 @@
         wait(zs.at[seven], rs_s)
         wait(pa.at[h, :, pl.ds(0, (NZ - 1) * SLOTS)], pa_s.at[h])
         for way in range(2):
-            for step in range(3):
+            for step in (0, 2):
                 wait(rf[h].at[0], ag_s.at[h, way, step])
             wait(rf[h].at[0, halves[way]], ag_s.at[h, way, 3])
-        columns = pl.ds(h * width, width)
-        wait(hlo.at[:, columns], h_s.at[0, h])
-        wait(hhi.at[:, columns], h_s.at[1, h])
+        for way in range(2):
+            wait(hlo.at[power_rows], h_s.at[way, NX])
+            for group in range(NX):
+                wait(hlo.at[pl.ds(0, pairs_rows)], h_s.at[way, group])
 
 
 def call(chunks, nc, cid, stack, pairs, order, refs):
@@ -504,7 +511,7 @@
             pltpu.VMEM((NX, CAP, ROWS, COLS), f32),
             dma((A_DEV, BLOCKS)), dma((A_DEV, nc)), dma((A_DEV, nc)), dma, dma, dma, dma((2,)), dma((2,)),
             dma, dma, dma, dma, dma((nc, 2, 4)), dma((nc, 2, 4)), dma((nc,)), dma((nc,)),
-            dma((2, nc)), dma((2, nc)), dma, dma, dma((A_DEV, nc)),
+            dma((2, NX + 1)), dma((2, NX + 1)), dma, dma, dma((A_DEV, nc)),
         ],
         compiler_params=pltpu.CompilerParams(
             collective_id=cid, has_side_effects=True, vmem_limit_bytes=48 << 20
@@ -514,17 +521,13 @@
 
 
 def local(stack, pairs, order, refs):
-    numbers = lax.broadcasted_iota(jnp.int32, (NACQ, NACQ), 0) // A_DEV
-    across = lax.broadcasted_iota(jnp.int32, (NACQ, NACQ), 1) // A_DEV
-    rows = lax.broadcast_in_dim(order, (NACQ, NACQ), (0,))
-    columns = lax.broadcast_in_dim(order, (NACQ, NACQ), (1,))
-    one = [refs[k] for k in range(NREF)]
-    held = (rows == one[0]) | (rows == one[1]) | (rows == one[2]) | (rows == one[3])
-    also = (columns == one[0]) | (columns == one[1]) | (columns == one[2]) | (columns == one[3])
-    together = jnp.sum((held & also & (numbers == across)).astype(jnp.int32))
+    numbers = jnp.arange(NACQ, dtype=jnp.int32)
+    slot = jnp.sum(jnp.where(order[None, :] == refs[:, None], numbers[None, :], 0), axis=1)
+    owner = slot // A_DEV
+    together = jnp.sum((owner[None, :] == owner[:, None]).astype(jnp.int32))
     pick = jnp.where(together > 8, 2, jnp.where(together > 4, 1, 0))
     variants = [functools.partial(call, 1, NC, 1), functools.partial(call, 2, NC, 2), functools.partial(call, 4, NC, 3)]
-    return lax.switch(pick, variants, stack, pairs, order, refs)
+    return lax.switch(pick, variants, stack, pairs.T, order, refs)
 
 
 NC = 1

time: 65.5 us -> 60.3 us (0.921)
  other arithmetic: 3.95 us -> 1.57 us
  local copies, waits for them, and re-layouts: 3.68 us -> 1.5 us
  Pallas kernels: 55.5 us -> 54.5 us
    and x1 -> x0, other arithmetic: 3.18 us -> none  [local(): numbers = lax.broadcasted_iota(jnp.int32, (NACQ, NACQ), 0) // A_DEV]
    slice x1 -> x0, local copies, waits for them, and re-layouts: 1.43 us -> none  [local(): one = [refs[k] for k in range(NREF)]]
    pallas_call x1, Pallas kernels: 55.5 us -> 54.5 us  [call(): pl.pallas_call(functools.partial(kernel, chunks, nc), out_shape=(jax.Shap...]
    reduce_sum x1 -> x2, other arithmetic: 0.77 us -> 1.56 us  [the longest x1 0.85 us: local(): jnp.sum(jnp.where(order[None, :] == refs[:, None], numbers[None, :], 0),...]
    another operation x1 -> x0, local copies, waits for them, and re-layouts: 0.76 us -> none
where the time goes in v3:
time: 60.3 us; the launch traced here: 59.5 us
  Pallas kernels  54.5 us (90%)
  between operations  1.94 us (3%)
  other arithmetic  1.57 us (3%)
  local copies, waits for them, and re-layouts  1.5 us (2%)
    pallas_call x1, Pallas kernels, call(): pl.pallas_call(functools.partial(kernel, chunks, nc), out_shape=(jax.Shap...  54.5 us
    unnamed x2, local copies, waits for them, and re-layouts  1.5 us

profile of v3, /device:TPU:1, one launch (start us, length us, event | category | flops | bytes accessed | tf_op | source)
XLA Modules:
  0.0 59.5 jit_solution(12593770412757744273)
XLA Ops:
  0.6 0.9 %select_reduce_fusion = s32[4]{0:T(128)S(1)} fusion(s32[128]{0:T(128)} %param.9, s32[4]{0:T(128)} %param.10), kind=kLoop, calls=%fused_computation.1 | loop fusion | flops 1532 | bytes 544 | tf_op jit(solution)/shard_map/reduce_sum | solution.py:525
  1.5 0.7 %convert_reduce_fusion = s32[]{:T(128)} fusion(s32[4]{0:T(128)S(1)} %and_select_fusion), kind=kLoop, calls=%fused_computation | loop fusion | flops 47 | bytes 20 | tf_op jit(solution)/shard_map/reduce_sum | solution.py:527
  3.5 54.5 %conditional.1 = ((f32[512,128]{1,0:T(8,128)S(1)}, f32[8,32,512]{2,1,0:T(8,128)S(1)})) conditional(s32[]{:T(128)} %clamp.3, (f32[4,2,128,512]{3,2,1,0:T(8,128)}, s32[2,8]{1,0:T(2,128)}, s32[128]{0:T(128)}, s32[4]{0:T(128)}) %tuple.31, (f32[4,2,128,512]{3,2,1,0:T(8,128)}, s32[2,8]{1,0:T(2,128)}, s32[128]{0:T(128)}, ...), branch_computations={%region_2.3_spmd, %region_3.4_spmd, %region_4.5_spmd} | conditional | bytes 8 | solution.py:530
  3.5 54.5 %sbas1.1 = (f32[512,128]{1,0:T(8,128)S(1)}, f32[8,32,512]{2,1,0:T(8,128)S(1)}) custom-call(f32[4,2,128,512]{3,2,1,0:T(8,128)} %get-tuple-element.49.stack_hbm, s32[2,8]{1,0:T(2,128)} %get-tuple-element.25.pairs, s32[128]{0:T(128)} %get-tuple-element.26.order, s32[4]{0:T(128)} %get-tuple-element.27.refs), custom_call_target="tpu_custom_call" | custom-call | tf_op jit(solution)/shard_map/cond/branch_0_fun/sbas1/pallas_call | solution.py:483
  58.0 0.7 %copy.23 = f32[512,128]{1,0:T(8,128)} copy(f32[512,128]{1,0:T(8,128)S(1)} %get-tuple-element.60) | data formatting | bytes 524288
  58.7 0.8 %copy.24 = f32[8,32,512]{2,1,0:T(8,128)} copy(f32[8,32,512]{2,1,0:T(8,128)S(1)} %get-tuple-element.61) | data formatting | bytes 1048576
  (1 shorter events, 0.0 us)

commit v4 on v3

--- a/solution.py
+++ b/solution.py
@@ -303,8 +303,8 @@
         where_ref.append(
             (lax.shift_right_logical(owner[k], 3), lax.rem(owner[k], NZ), jnp.minimum(rank, chunks - 1))
         )
+    scatter_x(where_ref)
     facts_around()
-    scatter_x(where_ref)
     wait(yx.at[three], y_s)
     for c in range(2, A_DEV):
         send_chunk(c, 0)
@@ -384,6 +384,13 @@
         keep(2 * SLOTS + NREF + s, total, full)
         return carry
 
+    def send_phases(part):
+        here = pl.ds(pl.multiple_of(z * pairs_rows, pairs_rows), pairs_rows)
+        for d in (4, 3, 5, 2, 6, 1, 7):
+            block = pl.ds(pl.multiple_of(at_z(d) * pairs_rows, pairs_rows), pairs_rows)
+            send(ph.at[part, :, block], pa.at[part, :, here], pa_s.at[part], pa_r.at[part], dev_z(d))
+        pa[part, :, here] = ph[part, :, here]
+
     order_d = (2, 1, 3, 0)
     for group in range(NX):
 
@@ -399,22 +406,20 @@
             keep(group * pairs_rows + CAP + index, imag, full)
             phase = jnp.where(live > 0, atan2(imag, real), 0.0)
             for b in range(BLOCKS):
-                ph[0, b, pl.ds(group * CAP + index, ROWS, stride=SLOTS), :] = phase[:, b * 128 : (b + 1) * 128]
+                ph[group // 2, b, pl.ds(group % 2 * CAP + index, ROWS, stride=pairs_rows), :] = phase[
+                    :, b * 128 : (b + 1) * 128
+                ]
             return carry
 
         lax.fori_loop(0, CAP, slot_body, 0)
         send_halo(group_rows(group), group)
-    for d in range(1, NZ):
-        target = at_z(d)
-        block = pl.ds(pl.multiple_of(target * SLOTS, SLOTS), SLOTS)
-        mine_there = pl.ds(pl.multiple_of(z * SLOTS, SLOTS), SLOTS)
-        send(ph.at[0, :, block], pa.at[0, :, mine_there], pa_s.at[0], pa_r.at[0], dev_z(d))
-    here = pl.ds(pl.multiple_of(z * SLOTS, SLOTS), SLOTS)
-    pa[0, :, here] = ph[0, :, here]
+        if group % 2 == 1:
+            send_phases(group // 2)
 
     lax.fori_loop(0, ACQS, power_body, 0)
     send_halo(power_rows, NX)
-    column_sums(0, QUANT)
+    column_sums(2 * SLOTS, NREF + ACQS)
+    column_sums(at_x(order_d[0]) * pairs_rows, pairs_rows)
     halo_here(power_rows, NX, QPAD - 2 * SLOTS)
 
     def power_box(t, carry):
@@ -429,6 +434,8 @@
     quarter = pl.ds(pl.multiple_of(x * ROWS, ROWS), ROWS)
     for d in order_d:
         group = at_x(d)
+        if d != order_d[0]:
+            column_sums(group * pairs_rows, pairs_rows)
 
         def coherence_body(t, carry, group=group):
             values = []
@@ -449,10 +456,15 @@
             send(coh.at[group], coherence.at[:, quarter, :], co_s, co_r, dev_x(d))
     coherence[:, quarter, :] = coh[x]
 
-    for h in range(nc):
-        wait(pa.at[h, :, pl.ds(0, (NZ - 1) * SLOTS)], pa_r.at[h])
-        for b in range(BLOCKS // nc):
-            series[pl.ds(h * width + b * 128, 128), :] = dot(pa[h, b], xt[...], ((0,), (0,)))
+    arrivals = pl.ds(0, (NZ - 1) * pairs_rows)
+    for part in range(2):
+        wait(pa.at[part, :, arrivals], pa_r.at[part])
+        weights = xt[...].reshape(NZ, SLOTS, NACQ)[:, part * pairs_rows : (part + 1) * pairs_rows]
+        weights = weights.reshape(NZ * pairs_rows, NACQ)
+        for b in range(BLOCKS):
+            rows_b = pl.ds(b * 128, 128)
+            term = dot(pa[part, b], weights, ((0,), (0,)))
+            series[rows_b, :] = term if part == 0 else series[rows_b, :] + term
 
     wait(coh.at[three], co_r)
     wait(coh.at[three], co_s)
@@ -463,7 +475,8 @@
         for c in range(A_DEV):
             sent(c, h)
         wait(zs.at[seven], rs_s)
-        wait(pa.at[h, :, pl.ds(0, (NZ - 1) * SLOTS)], pa_s.at[h])
+        for part in range(2):
+            wait(pa.at[part, :, arrivals], pa_s.at[part])
         for way in range(2):
             for step in (0, 2):
                 wait(rf[h].at[0], ag_s.at[h, way, step])
@@ -497,8 +510,8 @@
             pltpu.VMEM((NX, NREF, ROWS, COLS), f32),
             pltpu.VMEM((NX, NREF, ROWS, COLS), f32),
             [pltpu.VMEM((NZ, NREF, ROWS, width), f32)] * nc,
-            pltpu.VMEM((nc, BLOCKS // nc, ROWS * SLOTS, 128), f32),
-            pltpu.VMEM((nc, BLOCKS // nc, NZ * SLOTS, 128), f32),
+            pltpu.VMEM((2, BLOCKS, ROWS * SLOTS // 2, 128), f32),
+            pltpu.VMEM((2, BLOCKS, NZ * SLOTS // 2, 128), f32),
             pltpu.VMEM((NX, CAP, 128), jnp.int32),
             pltpu.SMEM((NX, CAP, 128), jnp.int32),
             pltpu.VMEM((NZ, NX, CAP, NACQ), f32),
@@ -510,7 +523,7 @@
             pltpu.VMEM((QPAD, COLS), f32),
             pltpu.VMEM((NX, CAP, ROWS, COLS), f32),
             dma((A_DEV, BLOCKS)), dma((A_DEV, nc)), dma((A_DEV, nc)), dma, dma, dma, dma((2,)), dma((2,)),
-            dma, dma, dma, dma, dma((nc, 2, 4)), dma((nc, 2, 4)), dma((nc,)), dma((nc,)),
+            dma, dma, dma, dma, dma((nc, 2, 4)), dma((nc, 2, 4)), dma((2,)), dma((2,)),
             dma((2, NX + 1)), dma((2, NX + 1)), dma, dma, dma((A_DEV, nc)),
         ],
         compiler_params=pltpu.CompilerParams(

time: 60.3 us -> 59.4 us (0.985); the launches traced: 59.5 us -> 59.3 us
  no operation moved by 1% of the time
where the time goes in v4:
time: 59.4 us; the launch traced here: 59.3 us
  Pallas kernels  54 us (91%)
  between operations  1.95 us (3%)
  other arithmetic  1.57 us (3%)
  local copies, waits for them, and re-layouts  1.5 us (3%)
    pallas_call x1, Pallas kernels, call(): pl.pallas_call(functools.partial(kernel, chunks, nc), out_shape=(jax.Shap...  54 us
    unnamed x2, local copies, waits for them, and re-layouts  1.5 us

profile of v4, /device:TPU:1, one launch (start us, length us, event | category | flops | bytes accessed | tf_op | source)
XLA Modules:
  0.0 59.3 jit_solution(8486142979212497021)
XLA Ops:
  0.6 0.9 %select_reduce_fusion = s32[4]{0:T(128)S(1)} fusion(s32[128]{0:T(128)} %param.9, s32[4]{0:T(128)} %param.10), kind=kLoop, calls=%fused_computation.1 | loop fusion | flops 1532 | bytes 544 | tf_op jit(solution)/shard_map/reduce_sum | solution.py:538
  1.5 0.7 %convert_reduce_fusion = s32[]{:T(128)} fusion(s32[4]{0:T(128)S(1)} %and_select_fusion), kind=kLoop, calls=%fused_computation | loop fusion | flops 47 | bytes 20 | tf_op jit(solution)/shard_map/reduce_sum | solution.py:540
  3.5 54.2 %conditional.1 = ((f32[512,128]{1,0:T(8,128)S(1)}, f32[8,32,512]{2,1,0:T(8,128)S(1)})) conditional(s32[]{:T(128)} %clamp.3, (f32[4,2,128,512]{3,2,1,0:T(8,128)}, s32[2,8]{1,0:T(2,128)}, s32[128]{0:T(128)}, s32[4]{0:T(128)}) %tuple.31, (f32[4,2,128,512]{3,2,1,0:T(8,128)}, s32[2,8]{1,0:T(2,128)}, s32[128]{0:T(128)}, ...), branch_computations={%region_2.3_spmd, %region_3.4_spmd, %region_4.5_spmd} | conditional | bytes 8 | solution.py:543
  3.5 54.0 %sbas1.1 = (f32[512,128]{1,0:T(8,128)S(1)}, f32[8,32,512]{2,1,0:T(8,128)S(1)}) custom-call(f32[4,2,128,512]{3,2,1,0:T(8,128)} %get-tuple-element.49.stack_hbm, s32[2,8]{1,0:T(2,128)} %get-tuple-element.25.pairs, s32[128]{0:T(128)} %get-tuple-element.26.order, s32[4]{0:T(128)} %get-tuple-element.27.refs), custom_call_target="tpu_custom_call" | custom-call | tf_op jit(solution)/shard_map/cond/branch_0_fun/sbas1/pallas_call | solution.py:496
  57.8 0.7 %copy.23 = f32[512,128]{1,0:T(8,128)} copy(f32[512,128]{1,0:T(8,128)S(1)} %get-tuple-element.60) | data formatting | bytes 524288
  58.5 0.8 %copy.24 = f32[8,32,512]{2,1,0:T(8,128)} copy(f32[8,32,512]{2,1,0:T(8,128)S(1)} %get-tuple-element.61) | data formatting | bytes 1048576
  (1 shorter events, 0.0 us)

commit v5 on v4

--- a/solution.py
+++ b/solution.py
@@ -217,7 +217,7 @@
             lax.fori_loop(0, NX, body, 0)
 
     def scatter():
-        for d in (4, 3, 5, 2, 6, 1, 7):
+        for d in (4, 5, 3, 6, 2, 7, 1):
             send(zs.at[at_z(d)], zr.at[z], rs_s, rs_r, dev_z(d))
         zr[z] = zs[z]
 

time: 59.4 us -> 59.4 us (level)
  no operation moved by 1% of the time
where the time goes in v5:
time: 59.4 us; the launch traced here: 59.3 us
  Pallas kernels  54 us (91%)
  between operations  1.95 us (3%)
  other arithmetic  1.57 us (3%)
  local copies, waits for them, and re-layouts  1.5 us (3%)
    pallas_call x1, Pallas kernels, call(): pl.pallas_call(functools.partial(kernel, chunks, nc), out_shape=(jax.Shap...  54 us
    unnamed x2, local copies, waits for them, and re-layouts  1.5 us

profile of v5, /device:TPU:1, one launch (start us, length us, event | category | flops | bytes accessed | tf_op | source)
XLA Modules:
  0.0 59.3 jit_solution(2138951542833375969)
XLA Ops:
  0.6 0.9 %select_reduce_fusion = s32[4]{0:T(128)S(1)} fusion(s32[128]{0:T(128)} %param.9, s32[4]{0:T(128)} %param.10), kind=kLoop, calls=%fused_computation.1 | loop fusion | flops 1532 | bytes 544 | tf_op jit(solution)/shard_map/reduce_sum | solution.py:538
  1.5 0.7 %convert_reduce_fusion = s32[]{:T(128)} fusion(s32[4]{0:T(128)S(1)} %and_select_fusion), kind=kLoop, calls=%fused_computation | loop fusion | flops 47 | bytes 20 | tf_op jit(solution)/shard_map/reduce_sum | solution.py:540
  3.5 54.2 %conditional.1 = ((f32[512,128]{1,0:T(8,128)S(1)}, f32[8,32,512]{2,1,0:T(8,128)S(1)})) conditional(s32[]{:T(128)} %clamp.3, (f32[4,2,128,512]{3,2,1,0:T(8,128)}, s32[2,8]{1,0:T(2,128)}, s32[128]{0:T(128)}, s32[4]{0:T(128)}) %tuple.31, (f32[4,2,128,512]{3,2,1,0:T(8,128)}, s32[2,8]{1,0:T(2,128)}, s32[128]{0:T(128)}, ...), branch_computations={%region_2.3_spmd, %region_3.4_spmd, %region_4.5_spmd} | conditional | bytes 8 | solution.py:543
  3.5 54.0 %sbas1.1 = (f32[512,128]{1,0:T(8,128)S(1)}, f32[8,32,512]{2,1,0:T(8,128)S(1)}) custom-call(f32[4,2,128,512]{3,2,1,0:T(8,128)} %get-tuple-element.49.stack_hbm, s32[2,8]{1,0:T(2,128)} %get-tuple-element.25.pairs, s32[128]{0:T(128)} %get-tuple-element.26.order, s32[4]{0:T(128)} %get-tuple-element.27.refs), custom_call_target="tpu_custom_call" | custom-call | tf_op jit(solution)/shard_map/cond/branch_0_fun/sbas1/pallas_call | solution.py:496
  57.8 0.7 %copy.23 = f32[512,128]{1,0:T(8,128)} copy(f32[512,128]{1,0:T(8,128)S(1)} %get-tuple-element.60) | data formatting | bytes 524288
  58.5 0.8 %copy.24 = f32[8,32,512]{2,1,0:T(8,128)} copy(f32[8,32,512]{2,1,0:T(8,128)S(1)} %get-tuple-element.61) | data formatting | bytes 1048576
  (1 shorter events, 0.0 us)
